TPU v7x, 512 devices: a whole 4x8x8 slice. The times are simulated.
512 devices in a mesh: img: 16 (over z, core), txt: 32 (over x, y).
Axes of the slice: x: 4, y: 8, z: 8, core: 2. Of those that a mesh axis runs over, the one named last changes fastest.
Arguments:
- images: bfloat16 [16384, 1024], P('img', 'txt'), may hold values from -4 to 4
- texts: bfloat16 [16384, 1024], P('txt', 'img'), may hold values from -4 to 4
- positive: int32 [16384], P('img'), may hold values from 0 to 16383, each once
- scale_logarithm: float32 [1], replicated, may hold values from 2.3 to 3
Outputs:
- loss: float32 [1], replicated
- grad_images: bfloat16 [16384, 1024], P('img', 'txt')
- grad_texts: bfloat16 [16384, 1024], P('txt', 'img')
- grad_log_scale: float32 [1], replicated
Inputs may be any that keep to these rules, and one draw needn't show every extreme that they name: `positive`: a permutation of 0 to 16383.
All inputs are finite; a program needn't handle non-finite values.
Results may differ from a plain program's by a relative error of at most 0.019.
Values may be sent and summed in bfloat16 or wider, within the bound.
No kernel may reach another device: no remote copies, remote signals or barrier semaphores. Data moves between devices by JAX's collectives and lax.ppermute only.
A program may use at most 64 MiB of HBM per device.

v0:
```python
import jax
import jax.numpy as jnp
from jax import lax
from jax.sharding import PartitionSpec as P


def per_device(images, texts, positive, scale_logarithm):
    logit_multiplier = jnp.exp(scale_logarithm[0])
    image_full = lax.all_gather(images, "txt", axis=1, tiled=True)
    text_full = lax.all_gather(texts, "img", axis=1, tiled=True)
    logit_matrix = logit_multiplier * lax.dot_general(
        image_full, text_full, (((1,), (1,)), ((), ())), preferred_element_type=jnp.float32
    )
    row_high = jnp.max(logit_matrix, axis=1)
    column_high = jnp.max(logit_matrix, axis=0)
    row_peak = lax.pmax(row_high, "txt")
    column_peak = lax.pmax(column_high, "img")
    row_total = lax.psum(jnp.sum(jnp.exp(logit_matrix - row_peak[:, None]), axis=1), "txt")
    column_total = lax.psum(jnp.sum(jnp.exp(logit_matrix - column_peak[None, :]), axis=0), "img")
    row_norms = row_peak + jnp.log(row_total)
    column_norms = column_peak + jnp.log(column_total)
    width_here = logit_matrix.shape[1]
    column_ids = lax.axis_index("txt") * width_here + jnp.arange(width_here, dtype=jnp.int32)
    matched = (positive[:, None] == column_ids[None, :]).astype(jnp.float32)
    weights = (
        0.5
        * (
            jnp.exp(logit_matrix - row_norms[:, None])
            + jnp.exp(logit_matrix - column_norms[None, :])
        )
        - matched
    )
    loss_part = 0.5 * (
        jnp.sum(row_norms) / lax.axis_size("txt") + jnp.sum(column_norms) / lax.axis_size("img")
    ) - jnp.sum(matched * logit_matrix)
    slope_part = jnp.sum(weights * logit_matrix)
    loss_total, slope_total = lax.psum((loss_part, slope_part), ("img", "txt"))
    batch_rows = logit_matrix.shape[0] * lax.axis_size("img")
    weights_reduced_precision = weights.astype(jnp.bfloat16)
    image_partial_loss = logit_multiplier * jnp.dot(
        weights_reduced_precision, text_full, preferred_element_type=jnp.float32
    )
    text_partial_loss = logit_multiplier * lax.dot_general(
        weights_reduced_precision,
        image_full,
        (((0,), (0,)), ((), ())),
        preferred_element_type=jnp.float32,
    )
    grad_images = lax.psum_scatter(
        image_partial_loss.astype(jnp.bfloat16), "txt", scatter_dimension=1, tiled=True
    )
    grad_texts = lax.psum_scatter(
        text_partial_loss.astype(jnp.bfloat16), "img", scatter_dimension=1, tiled=True
    )
    loss = (loss_total / batch_rows).reshape(1)
    grad_log_scale = (slope_total / batch_rows).reshape(1)
    return (loss, grad_images, grad_texts, grad_log_scale)


def solution(mesh):
    return jax.shard_map(
        per_device,
        mesh=mesh,
        in_specs=(P("img", "txt"), P("txt", "img"), P("img"), P()),
        out_specs=(P(), P("img", "txt"), P("txt", "img"), P()),
        check_vma=False,
    )
```

profile of v0, /device:TPU:1, one launch (start us, length us, event | category | flops | bytes accessed | tf_op | source)
XLA Modules:
  0.0 625.3 jit_solution(2454699020564901363)
XLA Ops:
  7.2 0.0 all-gather.5.cloned.1.call-start
  7.2 0.7 all-gather.5.cloned.1.call-update
  7.9 0.0 all-gather.3.cloned.1.call-start
  7.9 0.7 all-gather.3.cloned.1.call-update
  8.6 0.0 reduce-scatter.5.cloned.1.call-start
  9.4 48.6 %all-gather.5.cloned.1.call-done = bf16[512,1024]{0,1:T(8,128)(2,1)} async-done(((bf16[512,64]{0,1:T(8,128)(2,1)}), bf16[512,1024]{0,1:T(8,128)(2,1)}) %all-gather.5.cloned.1.call-update) | async-done | bytes 1048592 | tf_op jit(solution)/shard_map/all_gather | solution.py:10
  58.0 80.5 %all-gather.3.cloned.1.call-done = bf16[1024,1024]{0,1:T(8,128)(2,1)} async-done(((bf16[1024,32]{0,1:T(8,128)(2,1)}), bf16[1024,1024]{0,1:T(8,128)(2,1)}) %all-gather.3.cloned.1.call-update) | async-done | bytes 2097168 | tf_op jit(solution)/shard_map/all_gather | solution.py:9
  138.5 3.2 fusion.5
  141.7 0.0 copy-start
  141.7 28.4 %pmax.15 = f32[512]{0:T(512)S(1)} all-reduce(f32[512]{0:T(512)S(1)} %get-tuple-element.8), channel_id=1, replica_groups=mesh['img'=16,'txt'=32] {'img'}, use_global_device_ids=true, to_apply=%region_6.0 | all-reduce | flops 512 | bytes 4096 | tf_op jit(solution)/shard_map/pmax | solution.py:17
  170.2 57.9 %pmax.14 = f32[1024]{0:T(1024)S(1)} all-reduce(f32[1024]{0:T(1024)S(1)} %get-tuple-element.9), channel_id=1, replica_groups=mesh['img'=16,'txt'=32] {'txt'}, use_global_device_ids=true, to_apply=%region_1.0 | all-reduce | flops 1024 | bytes 8192 | tf_op jit(solution)/shard_map/pmax | solution.py:16
  228.1 1.0 exponential_reduce_fusion
  229.1 37.0 %psum.29 = f32[512]{0:T(512)S(1)} all-reduce(f32[512]{0:T(512)S(1)} %get-tuple-element.6), channel_id=1, replica_groups=mesh['img'=16,'txt'=32] {'img'}, use_global_device_ids=true, to_apply=%region_8.0 | all-reduce | flops 512 | bytes 4096 | tf_op jit(solution)/shard_map/psum | solution.py:19
  266.1 0.6 fusion.6
  266.7 55.7 %psum.28 = f32[1024]{0:T(1024)S(1)} all-reduce(f32[1024]{0:T(1024)S(1)} %get-tuple-element.7), channel_id=1, replica_groups=mesh['img'=16,'txt'=32] {'txt'}, use_global_device_ids=true, to_apply=%region_3.0 | all-reduce | flops 1024 | bytes 8192 | tf_op jit(solution)/shard_map/psum | solution.py:18
  322.4 0.6 fusion.7
  323.0 0.0 copy-done
  323.0 0.0 copy-start.1
  323.0 4.2 multiply_convert_fusion.1
  327.2 0.0 reduce-scatter.5.cloned.1.call-update
  327.2 0.0 reduce-scatter.3.cloned.1.call-start
  327.3 0.0 copy-done.1
  327.3 3.7 multiply_convert_fusion
  331.0 0.0 reduce-scatter.3.cloned.1.call-update
  332.3 2.3 multiply_reduce_fusion
  335.3 109.8 %all-reduce = (f32[]{:T(128)}, f32[]{:T(128)}) all-reduce(f32[]{:T(128)S(6)} %sub.42, f32[]{:T(128)} %get-tuple-element.4), channel_id=1, replica_groups=mesh['img'=16,'txt'=32] {'img','txt'}, use_global_device_ids=true, to_apply=%region_11.0 | all-reduce | flops 2 | bytes 16 | tf_op jit(solution)/shard_map/psum | solution.py:37
  446.4 0.0 reduce-scatter.5.cloned.1.call-done
  446.5 170.1 %reduce-scatter.3.cloned.1.call-done = bf16[1024,32]{0,1:T(8,128)(2,1)} async-done(((bf16[1024,1024]{0,1:T(8,128)(2,1)}), bf16[1024,32]{0,1:T(8,128)(2,1)}) %reduce-scatter.3.cloned.1.call-update) | async-done | bytes 65552 | tf_op jit(solution)/shard_map/reduce_scatter | solution.py:49
  (1 shorter events, 0.0 us)
Async XLA Ops:
  7.2 50.8 %all-gather.5.cloned.1.call-start = ((), (), s32[]{:S(2)}) async-start(), calls=%async_computation.3 | async-start | bytes 1114112 | tf_op jit(solution)/shard_map/all_gather | solution.py:10
  7.9 130.6 %all-gather.3.cloned.1.call-start = ((), (), s32[]{:S(2)}) async-start(), calls=%async_computation.2 | async-start | bytes 2162688 | tf_op jit(solution)/shard_map/all_gather | solution.py:9
  8.6 437.8 %reduce-scatter.5.cloned.1.call-start = ((), (), s32[]{:S(2)}) async-start(), calls=%async_computation.5 | async-start | bytes 1114112 | tf_op jit(solution)/shard_map/reduce_scatter | solution.py:52
  141.7 181.3 %copy-start = (s32[1024]{0:T(1024)S(1)}, s32[1024]{0:T(1024)}, u32[]{:S(2)}) copy-start(s32[1024]{0:T(1024)} %param.6) | copy-start | bytes 12292
  323.0 4.3 copy-start.1
  327.2 289.3 %reduce-scatter.3.cloned.1.call-start = ((), (), s32[]{:S(2)}) async-start(), calls=%async_computation.4 | async-start | bytes 2162688 | tf_op jit(solution)/shard_map/reduce_scatter | solution.py:49
Sparse Core Ops, SparseCore 0:
  10.1 47.8 all-gather.4
  61.2 77.2 all-gather.2
  327.4 66.6 reduce-scatter.4
  399.5 216.9 reduce-scatter.2
where the time goes:
time: 630 us; the launch traced here: 625 us
  waiting for transfers between devices  301 us (48%)
  blocking collectives  289 us (46%)
  between operations  20 us (3%)
  matrix products  11.1 us (2%)
    reduce_scatter x1, waiting for transfers between devices, per_device(): lax.psum_scatter(image_partial_loss.astype(jnp.bfloat16), 'txt', scatter_...  170 us
    psum x1, blocking collectives, per_device(): loss_total, slope_total = lax.psum((loss_part, slope_part), ('img', 'txt'))  110 us
    all_gather x1, waiting for transfers between devices, per_device(): image_full = lax.all_gather(images, 'txt', axis=1, tiled=True)  80.5 us
    pmax x1, blocking collectives, per_device(): row_peak = lax.pmax(row_high, 'txt')  57.9 us
    psum x1, blocking collectives, per_device(): lax.psum(jnp.sum(jnp.exp(logit_matrix - row_peak[:, None]), axis=1), 'txt')  55.7 us
    all_gather x1, waiting for transfers between devices, per_device(): text_full = lax.all_gather(texts, 'img', axis=1, tiled=True)  48.6 us
    psum x1, blocking collectives, per_device(): lax.psum(jnp.sum(jnp.exp(logit_matrix - column_peak[None, :]), axis=0), '...  37 us
    pmax x1, blocking collectives, per_device(): column_peak = lax.pmax(column_high, 'img')  28.4 us
  transfers between devices with their start and end apart: 4, of which 3 were waited for; matrix products, arithmetic and copies ran while one was open for 1% of the time, Pallas kernels for 0%

commit v1 on v0

v1 whole, which is shorter than its diff:
```python
import jax
import jax.numpy as jnp
from jax import lax
from jax.sharding import PartitionSpec as P

X_CHIPS = 4
Y_CHIPS = 8
ALONG_Y = [[x * Y_CHIPS + y for y in range(Y_CHIPS)] for x in range(X_CHIPS)]
ALONG_X = [[x * Y_CHIPS + y for x in range(X_CHIPS)] for y in range(Y_CHIPS)]


def exchange(blocks, axis, groups=None):
    return lax.all_to_all(blocks, axis, 0, 0, axis_index_groups=groups)


def collect(block, axis, count, groups=None):
    return exchange(jnp.broadcast_to(block[None], (count,) + block.shape), axis, groups)


def local_softmax(logits, axis):
    high = jnp.max(logits, axis=axis, keepdims=True)
    powers = jnp.exp(logits - high)
    total = jnp.sum(powers, axis=axis)
    mean = jnp.sum(powers * logits, axis=axis) / total
    return jnp.squeeze(high, axis) + jnp.log(total), mean


def merge(norms, means):
    high = jnp.max(norms, axis=0)
    powers = jnp.exp(norms - high)
    total = jnp.sum(powers, axis=0)
    return high + jnp.log(total), jnp.sum(jnp.sum(powers * means, axis=0) / total)


def per_device(images, texts, positive, scale_logarithm):
    n_img, n_txt = lax.axis_size("img"), lax.axis_size("txt")
    rows, cols = images.shape[0], texts.shape[0]
    width = images.shape[1] * n_txt
    scale = jnp.exp(scale_logarithm[0])

    text_full = lax.all_gather(texts, "img", axis=1, tiled=True)
    by_y = collect(images.T, "txt", Y_CHIPS, ALONG_Y)
    image_t = collect(by_y, "txt", X_CHIPS, ALONG_X).reshape(width, rows)

    logits = scale * lax.dot_general(
        image_t, text_full, (((0,), (1,)), ((), ())), preferred_element_type=jnp.float32
    )
    column_ids = lax.axis_index("txt") * cols + jnp.arange(cols, dtype=jnp.int32)
    matched = (positive[:, None] == column_ids[None, :]).astype(jnp.float32)

    col_norm, col_mean = local_softmax(logits, 0)
    row_norm, row_mean = local_softmax(logits, 1)
    matched_sum = jnp.sum(matched * logits)

    packed = jnp.concatenate([col_norm, col_mean, jnp.full((128,), matched_sum)])
    seen = collect(packed[None], "img", n_img)[:, 0]
    column_norms, col_slope = merge(seen[:, :cols], seen[:, cols : 2 * cols])
    matched_here = jnp.sum(seen[:, 2 * cols])
    col_loss = 0.5 * jnp.sum(column_norms) - matched_here
    col_slope = 0.5 * col_slope - matched_here

    packed = jnp.concatenate(
        [row_norm, row_mean, jnp.full((128,), col_loss), jnp.full((128,), col_slope)]
    )
    seen = collect(packed[None], "txt", n_txt)[:, 0]
    row_norms, row_slope = merge(seen[:, :rows], seen[:, rows : 2 * rows])
    col_loss_all = jnp.sum(seen[:, 2 * rows])
    col_slope_all = jnp.sum(seen[:, 2 * rows + 128])

    packed = jnp.concatenate(
        [jnp.full((128,), 0.5 * jnp.sum(row_norms)), jnp.full((128,), 0.5 * row_slope)]
    )
    seen = collect(packed[None], "img", n_img)[:, 0]
    batch = rows * n_img
    loss = ((jnp.sum(seen[:, 0]) + col_loss_all) / batch).reshape(1)
    grad_log_scale = ((jnp.sum(seen[:, 128]) + col_slope_all) / batch).reshape(1)

    weights = (
        0.5 * (jnp.exp(logits - row_norms[:, None]) + jnp.exp(logits - column_norms[None, :]))
        - matched
    ).astype(jnp.bfloat16)

    text_part = scale * lax.dot_general(
        weights, image_t, (((0,), (1,)), ((), ())), preferred_element_type=jnp.float32
    )
    grad_texts = lax.psum_scatter(
        text_part.astype(jnp.bfloat16), "img", scatter_dimension=1, tiled=True
    )

    image_part = scale * lax.dot_general(
        text_full, weights, (((0,), (1,)), ((), ())), preferred_element_type=jnp.float32
    )
    image_part = image_part.astype(jnp.bfloat16).reshape(X_CHIPS, width // X_CHIPS, rows)
    over_x = exchange(image_part, "txt", ALONG_X)
    over_x = jnp.sum(over_x.astype(jnp.float32), axis=0).astype(jnp.bfloat16)
    over_y = exchange(over_x.reshape(Y_CHIPS, -1, rows), "txt", ALONG_Y)
    grad_images = jnp.sum(over_y.astype(jnp.float32), axis=0).astype(jnp.bfloat16).T
    return (loss, grad_images, grad_texts, grad_log_scale)


def solution(mesh):
    return jax.shard_map(
        per_device,
        mesh=mesh,
        in_specs=(P("img", "txt"), P("txt", "img"), P("img"), P()),
        out_specs=(P(), P("img", "txt"), P("txt", "img"), P()),
        check_vma=False,
    )
```

time: 630 us -> 193 us (0.31)
  blocking collectives: 289 us -> 13.9 us
  waiting for transfers between devices: 301 us -> 86.9 us
  starting transfers between devices: 0.16 us -> 41 us
  local copies, waits for them, and re-layouts: 0.01 us -> 6.81 us
    psum x3 -> x0, blocking collectives: 203 us -> none  [the longest x1 110 us: per_device(): loss_total, slope_total = lax.psum((loss_part, slope_part), ('img', 'txt'))]
    reduce_scatter x2 -> x1, waiting for transfers between devices: 170 us -> 0.01 us  [per_device(): lax.psum_scatter(text_part.astype(jnp.bfloat16), 'img', scatter_dimension...]
    pmax x2 -> x0, blocking collectives: 86.4 us -> none  [the longest x1 57.9 us: per_device(): row_peak = lax.pmax(row_high, 'txt')]
    all_gather x1 -> x0, waiting for transfers between devices: 80.5 us -> none  [per_device(): image_full = lax.all_gather(images, 'txt', axis=1, tiled=True)]
    all_to_all x0 -> x6, waiting for transfers between devices: none -> 60.1 us  [exchange(): return lax.all_to_all(blocks, axis, 0, 0, axis_index_groups=groups)]
    all_to_all x0 -> x6, starting transfers between devices: none -> 41 us  [exchange(): return lax.all_to_all(blocks, axis, 0, 0, axis_index_groups=groups)]
    all_gather x1, waiting for transfers between devices: 48.6 us -> 26.1 us  [per_device(): text_full = lax.all_gather(texts, 'img', axis=1, tiled=True)]
    all_to_all x0 -> x1, blocking collectives: none -> 13.9 us  [exchange(): return lax.all_to_all(blocks, axis, 0, 0, axis_index_groups=groups)]
  transfers between devices with their start and end apart: 4 -> 8, of which waited for: 3 -> 6; matrix products, arithmetic and copies ran while one was open for 1% -> 5% of each run, Pallas kernels for 0% -> 0%
where the time goes in v1:
time: 193 us; the launch traced here: 192 us
  waiting for transfers between devices  86.9 us (45%)
  starting transfers between devices  41 us (21%)
  between operations  23.7 us (12%)
  blocking collectives  13.9 us (7%)
  matrix products  11.7 us (6%)
  other arithmetic  7.88 us (4%)
  local copies, waits for them, and re-layouts  6.81 us (4%)
    all_to_all x6, waiting for transfers between devices, exchange(): return lax.all_to_all(blocks, axis, 0, 0, axis_index_groups=groups)  60.1 us
    all_to_all x6, starting transfers between devices, exchange(): return lax.all_to_all(blocks, axis, 0, 0, axis_index_groups=groups)  41 us
    all_gather x1, waiting for transfers between devices, per_device(): text_full = lax.all_gather(texts, 'img', axis=1, tiled=True)  26.1 us
    all_to_all x1, blocking collectives, exchange(): return lax.all_to_all(blocks, axis, 0, 0, axis_index_groups=groups)  13.9 us
    broadcast_in_dim x5, local copies, waits for them, and re-layouts, collect(): jnp.broadcast_to(block[None], (count,) + block.shape)  4.75 us
    dot_general x1, matrix products, per_device(): lax.dot_general(weights, image_t, (((0,), (1,)), ((), ())), preferred_ele...  4.75 us
  transfers between devices with their start and end apart: 8, of which 6 were waited for; matrix products, arithmetic and copies ran while one was open for 5% of the time, Pallas kernels for 0%

profile of v1, /device:TPU:1, one launch (start us, length us, event | category | flops | bytes accessed | tf_op | source)
XLA Modules:
  0.0 191.8 jit_solution(5257704667701318652)
XLA Ops:
  7.2 1.7 broadcast_in_dim.18
  8.9 7.7 %all-to-all-start = ((bf16[8,32,1024]{2,1,0:T(8,128)(2,1)}), bf16[8,32,1024]{2,1,0:T(8,128)(2,1)S(1)}, u32[]{:S(2)}, u32[]{:S(2)}) async-start(bf16[8,32,1024]{2,1,0:T(8,128)(2,1)} %broadcast_in_dim.18), calls=%async_computation | async-start | bytes 1048576 | tf_op jit(solution)/shard_map/all_to_all | solution.py:13
  16.5 0.0 all-gather.2.cloned.1.call-start
  16.5 0.7 all-gather.2.cloned.1.call-update
  17.2 14.0 %all-to-all-done = bf16[8,32,1024]{2,1,0:T(8,128)(2,1)S(1)} async-done(((bf16[8,32,1024]{2,1,0:T(8,128)(2,1)}), bf16[8,32,1024]{2,1,0:T(8,128)(2,1)S(1)}, u32[]{:S(2)}, u32[]{:S(2)}) %all-to-all-start) | async-done | bytes 524320 | tf_op jit(solution)/shard_map/all_to_all | solution.py:13
  31.3 1.6 broadcast_in_dim.19
  32.9 7.2 %all-to-all-start.1 = ((bf16[4,8,32,1024]{3,2,1,0:T(8,128)(2,1)}), bf16[4,8,32,1024]{3,2,1,0:T(8,128)(2,1)S(1)}, u32[]{:S(2)}, u32[]{:S(2)}) async-start(bf16[4,8,32,1024]{3,2,1,0:T(8,128)(2,1)} %broadcast_in_dim.19), calls=%async_computation.1 | async-start | bytes 4194304 | tf_op jit(solution)/shard_map/all_to_all | solution.py:13
  40.8 26.1 %all-gather.2.cloned.1.call-done = bf16[512,1024]{0,1:T(8,128)(2,1)} async-done(((bf16[512,64]{0,1:T(8,128)(2,1)}), bf16[512,1024]{0,1:T(8,128)(2,1)}) %all-gather.2.cloned.1.call-update) | async-done | bytes 1048592 | tf_op jit(solution)/shard_map/all_gather | solution.py:41
  66.9 0.0 all-to-all-done.1
  66.9 0.0 copy-start.1
  66.9 1.4 copy-done.1
  68.3 0.0 copy-start.2
  68.3 3.2 %fusion.11 = (f32[1024]{0:T(1024)S(1)}, f32[512]{0:T(512)S(1)}, f32[1024,512]{1,0:T(8,128)S(1)}) fusion(bf16[1024,1024]{1,0:T(8,128)(2,1)} %bitcast.23, bf16[512,1024]{0,1:T(8,128)(2,1)} %all-gather.2.cloned.1.call-done, f32[]{:T(128)} %bitcast), kind=kOutput, calls=%fused_computation.41 | convolution fusion | flops 1075313152 | bytes 5249028 | tf_op jit(solution)/shard_map/dot_general | solution.py:45
  71.5 0.0 copy-start
  71.5 0.0 copy-done.2
  71.6 0.0 copy-start.3
  71.6 2.6 %fusion.4 = (f32[1024]{0:T(1024)S(1)}, f32[1024]{0:T(1024)S(1)}, f32[]{:T(128)}, f32[512]{0:T(512)S(1)}, f32[512]{0:T(512)S(1)}) fusion(f32[1024,512]{1,0:T(8,128)S(1)} %get-tuple-element.31, f32[1024]{0:T(1024)S(1)} %get-tuple-element.11, s32[512]{0:T(512)S(1)} %iota_add_fusion, s32[1024]{0:T(1024)S(1)} %copy-done.2, f32[512]{0:T(512)S(1)} %get-tuple-element.12), kind=kLoop, calls=%fused_computation.12 | loop fusion | flops 5764095 | bytes 2121732 | tf_op jit(solution)/shard_map/reduce_sum | solution.py:23
  74.2 0.7 broadcast_in_dim.20
  74.9 0.7 broadcast_in_dim.21
  75.5 10.8 %all-to-all-start.2 = ((f32[16,1,1152]{2,1,0:T(1,128)}), f32[16,1,1152]{2,1,0:T(1,128)S(1)}, u32[]{:S(2)}, u32[]{:S(2)}) async-start(f32[16,1,1152]{2,1,0:T(1,128)} %broadcast_in_dim.21), calls=%async_computation.2 | async-start | bytes 147456 | tf_op jit(solution)/shard_map/all_to_all | solution.py:13
  86.3 8.0 %all-to-all-done.2 = f32[16,1,1152]{2,1,0:T(1,128)S(1)} async-done(((f32[16,1,1152]{2,1,0:T(1,128)}), f32[16,1,1152]{2,1,0:T(1,128)S(1)}, u32[]{:S(2)}, u32[]{:S(2)}) %all-to-all-start.2) | async-done | bytes 73760 | tf_op jit(solution)/shard_map/all_to_all | solution.py:13
  94.3 0.6 slice_reduce_fusion.6
  94.9 0.6 fusion.13
  98.2 0.2 broadcast_in_dim.24
  98.3 13.9 %all_to_all.35 = f32[32,1,2304]{2,1,0:T(1,128)S(1)} all-to-all(f32[32,1,2304]{2,1,0:T(1,128)S(1)} %broadcast_in_dim.24), channel_id=1, replica_groups=mesh['img'=16,'txt'=32] {'txt'}, dimensions={0} | all-to-all | bytes 589824 | tf_op jit(solution)/shard_map/all_to_all | solution.py:13
  112.3 0.6 fusion.12
  112.9 0.0 copy-done
  112.9 0.0 copy-done.3
  112.9 3.7 %multiply_convert_fusion = bf16[1024,1024]{0,1:T(8,128)(2,1)} fusion(bf16[512,1024]{0,1:T(8,128)(2,1)S(1)} %copy-done.3, f32[]{:T(128)} %bitcast, f32[1024,512]{1,0:T(8,128)S(1)} %get-tuple-element.31, f32[512]{0:T(512)S(1)} %get-tuple-element.24, f32[1024]{0:T(1024)S(1)} %get-tuple-element.22, s32[512]{0:T(512)S(1)} %iota_add_fusion, s32[1024]{0:T(1024)S(1)} %copy-done.2), kind=kOutput, calls=%fused_computation | convolution fusion | flops 1080033280 | bytes 5255172 | tf_op jit(solution)/shard_map/dot_general | solution.py:90
  116.6 3.6 %all-to-all-start.5 = ((bf16[4,256,1024]{2,1,0:T(8,128)(2,1)}), bf16[4,256,1024]{2,1,0:T(8,128)(2,1)S(1)}, u32[]{:S(2)}, u32[]{:S(2)}) async-start(bf16[4,256,1024]{2,1,0:T(8,128)(2,1)} %bitcast.25), calls=%async_computation.5 | async-start | bytes 4194304 | tf_op jit(solution)/shard_map/all_to_all | solution.py:13
  120.2 0.0 reduce-scatter.2.cloned.1.call-start
  120.3 4.7 %multiply_convert_fusion.1 = bf16[512,1024]{0,1:T(8,128)(2,1)} fusion(bf16[1024,1024]{1,0:T(8,128)(2,1)} %bitcast.24, f32[]{:T(128)} %bitcast, f32[1024,512]{1,0:T(8,128)} %copy-done, f32[512]{0:T(512)S(1)} %get-tuple-element.24, f32[1024]{0:T(1024)S(1)} %get-tuple-element.22, s32[512]{0:T(512)S(1)} %iota_add_fusion, s32[1024]{0:T(1024)S(1)} %copy-done.2), kind=kOutput, calls=%fused_computation.6 | convolution fusion | flops 1078984704 | bytes 5255172 | tf_op jit(solution)/shard_map/dot_general | solution.py:83
  125.0 0.0 reduce-scatter.2.cloned.1.call-update
  126.4 18.0 %all-to-all-done.5 = bf16[4,256,1024]{2,1,0:T(8,128)(2,1)S(1)} async-done(((bf16[4,256,1024]{2,1,0:T(8,128)(2,1)}), bf16[4,256,1024]{2,1,0:T(8,128)(2,1)S(1)}, u32[]{:S(2)}, u32[]{:S(2)}) %all-to-all-start.5) | async-done | bytes 2097184 | tf_op jit(solution)/shard_map/all_to_all | solution.py:13
  144.3 0.6 broadcast_in_dim.26
  144.9 6.4 %all-to-all-start.4 = ((f32[16,1,256]{2,1,0:T(1,128)}), f32[16,1,256]{2,1,0:T(1,128)S(1)}, u32[]{:S(2)}, u32[]{:S(2)}) async-start(f32[16,1,256]{2,1,0:T(1,128)} %broadcast_in_dim.26), calls=%async_computation.4 | async-start | bytes 32768 | tf_op jit(solution)/shard_map/all_to_all | solution.py:13
  151.4 1.3 reduce_sum.202
  152.7 6.1 %all-to-all-done.4 = f32[16,1,256]{2,1,0:T(1,128)S(1)} async-done(((f32[16,1,256]{2,1,0:T(1,128)}), f32[16,1,256]{2,1,0:T(1,128)S(1)}, u32[]{:S(2)}, u32[]{:S(2)}) %all-to-all-start.4) | async-done | bytes 16416 | tf_op jit(solution)/shard_map/all_to_all | solution.py:13
  158.8 5.3 %all-to-all-start.6 = ((bf16[8,32,1024]{2,1,0:T(8,128)(2,1)}), bf16[8,32,1024]{2,1,0:T(8,128)(2,1)S(1)}, u32[]{:S(2)}, u32[]{:S(2)}) async-start(bf16[8,32,1024]{2,1,0:T(8,128)(2,1)} %bitcast.6), calls=%async_computation.6 | async-start | bytes 1048576 | tf_op jit(solution)/shard_map/all_to_all | solution.py:13
  164.1 0.7 slice_reduce_fusion.2
  164.8 0.6 slice_reduce_fusion.4
  168.0 14.0 %all-to-all-done.6 = bf16[8,32,1024]{2,1,0:T(8,128)(2,1)S(1)} async-done(((bf16[8,32,1024]{2,1,0:T(8,128)(2,1)}), bf16[8,32,1024]{2,1,0:T(8,128)(2,1)S(1)}, u32[]{:S(2)}, u32[]{:S(2)}) %all-to-all-start.6) | async-done | bytes 524320 | tf_op jit(solution)/shard_map/all_to_all | solution.py:13
  182.0 0.7 reduce_sum.203
  182.7 0.0 reduce-scatter.2.cloned.1.call-done
  (16 shorter events, 0.2 us)
Async XLA Ops:
  8.9 22.4 %all-to-all-start = ((bf16[8,32,1024]{2,1,0:T(8,128)(2,1)}), bf16[8,32,1024]{2,1,0:T(8,128)(2,1)S(1)}, u32[]{:S(2)}, u32[]{:S(2)}) async-start(bf16[8,32,1024]{2,1,0:T(8,128)(2,1)} %broadcast_in_dim.18), calls=%async_computation | async-start | bytes 1048576 | tf_op jit(solution)/shard_map/all_to_all | solution.py:13
  16.5 50.4 %all-gather.2.cloned.1.call-start = ((), (), s32[]{:S(2)}) async-start(), calls=%async_computation.8 | async-start | bytes 1114112 | tf_op jit(solution)/shard_map/all_gather | solution.py:41
  32.9 34.1 %all-to-all-start.1 = ((bf16[4,8,32,1024]{3,2,1,0:T(8,128)(2,1)}), bf16[4,8,32,1024]{3,2,1,0:T(8,128)(2,1)S(1)}, u32[]{:S(2)}, u32[]{:S(2)}) async-start(bf16[4,8,32,1024]{3,2,1,0:T(8,128)(2,1)} %broadcast_in_dim.19), calls=%async_computation.1 | async-start | bytes 4194304 | tf_op jit(solution)/shard_map/all_to_all | solution.py:13
  66.9 1.4 copy-start.1
  68.3 3.2 %copy-start.2 = (s32[1024]{0:T(1024)S(1)}, s32[1024]{0:T(1024)}, u32[]{:S(2)}) copy-start(s32[1024]{0:T(1024)} %param.6) | copy-start | bytes 12292
  71.5 41.4 %copy-start = (f32[1024,512]{1,0:T(8,128)}, f32[1024,512]{1,0:T(8,128)S(1)}, u32[]{:S(2)}) copy-start(f32[1024,512]{1,0:T(8,128)S(1)} %get-tuple-element.31) | copy-start | bytes 6291460
  71.6 41.4 %copy-start.3 = (bf16[512,1024]{0,1:T(8,128)(2,1)S(1)}, bf16[512,1024]{0,1:T(8,128)(2,1)}, u32[]{:S(2)}) copy-start(bf16[512,1024]{0,1:T(8,128)(2,1)} %all-gather.2.cloned.1.call-done) | copy-start | bytes 3145732
  75.5 18.7 %all-to-all-start.2 = ((f32[16,1,1152]{2,1,0:T(1,128)}), f32[16,1,1152]{2,1,0:T(1,128)S(1)}, u32[]{:S(2)}, u32[]{:S(2)}) async-start(f32[16,1,1152]{2,1,0:T(1,128)} %broadcast_in_dim.21), calls=%async_computation.2 | async-start | bytes 147456 | tf_op jit(solution)/shard_map/all_to_all | solution.py:13
  116.6 27.7 %all-to-all-start.5 = ((bf16[4,256,1024]{2,1,0:T(8,128)(2,1)}), bf16[4,256,1024]{2,1,0:T(8,128)(2,1)S(1)}, u32[]{:S(2)}, u32[]{:S(2)}) async-start(bf16[4,256,1024]{2,1,0:T(8,128)(2,1)} %bitcast.25), calls=%async_computation.5 | async-start | bytes 4194304 | tf_op jit(solution)/shard_map/all_to_all | solution.py:13
  120.2 62.5 %reduce-scatter.2.cloned.1.call-start = ((), (), s32[]{:S(2)}) async-start(), calls=%async_computation.9 | async-start | bytes 1114112 | tf_op jit(solution)/shard_map/reduce_scatter | solution.py:86
  144.9 13.8 %all-to-all-start.4 = ((f32[16,1,256]{2,1,0:T(1,128)}), f32[16,1,256]{2,1,0:T(1,128)S(1)}, u32[]{:S(2)}, u32[]{:S(2)}) async-start(f32[16,1,256]{2,1,0:T(1,128)} %broadcast_in_dim.26), calls=%async_computation.4 | async-start | bytes 32768 | tf_op jit(solution)/shard_map/all_to_all | solution.py:13
  158.8 23.3 %all-to-all-start.6 = ((bf16[8,32,1024]{2,1,0:T(8,128)(2,1)}), bf16[8,32,1024]{2,1,0:T(8,128)(2,1)S(1)}, u32[]{:S(2)}, u32[]{:S(2)}) async-start(bf16[8,32,1024]{2,1,0:T(8,128)(2,1)} %bitcast.6), calls=%async_computation.6 | async-start | bytes 1048576 | tf_op jit(solution)/shard_map/all_to_all | solution.py:13
Sparse Core Ops, SparseCore 0:
  19.5 47.4 all-gather.1
  125.2 54.3 reduce-scatter.1

commit v2 on v1

v2 whole, which is shorter than its diff:
```python
import jax
import jax.numpy as jnp
from jax import lax
from jax.sharding import PartitionSpec as P

X_CHIPS = 4
Y_PAIRS = 4
CORES = 2
PAIRS = [
    [(x * Y_PAIRS + pair) * 2 + side for pair in range(Y_PAIRS)]
    for x in range(X_CHIPS)
    for side in range(2)
]
SQUARES = [
    [(x * Y_PAIRS + pair) * 2 + side for x in range(X_CHIPS) for side in range(2)]
    for pair in range(Y_PAIRS)
]
BOTH_CORES = [[z * CORES + core for core in range(CORES)] for z in range(8)]
ALONG_Z = [[z * CORES + core for z in range(8)] for core in range(CORES)]


def exchange(blocks, axis, groups=None):
    return lax.all_to_all(blocks, axis, 0, 0, axis_index_groups=groups)


def collect(block, axis, count, groups=None):
    return exchange(jnp.broadcast_to(block[None], (count,) + block.shape), axis, groups)


def local_softmax(logits, axis):
    high = jnp.max(logits, axis=axis, keepdims=True)
    powers = jnp.exp(logits - high)
    total = jnp.sum(powers, axis=axis)
    mean = jnp.sum(powers * logits, axis=axis) / total
    return jnp.squeeze(high, axis) + jnp.log(total), mean


def merge(norms):
    high = jnp.max(norms, axis=0)
    return high + jnp.log(jnp.sum(jnp.exp(norms - high), axis=0))


def per_device(images, texts, positive, scale_logarithm):
    n_img, n_txt = lax.axis_size("img"), lax.axis_size("txt")
    rows, cols = images.shape[0], texts.shape[0]
    width = images.shape[1] * n_txt
    scale = jnp.exp(scale_logarithm[0])

    by_core = collect(texts.T, "img", CORES, BOTH_CORES).reshape(-1, cols)
    text_t = lax.all_gather(by_core, "img", axis=0, axis_index_groups=ALONG_Z, tiled=True)
    by_pair = collect(images.T, "txt", Y_PAIRS, PAIRS)
    by_square = collect(by_pair, "txt", 2 * X_CHIPS, SQUARES)
    image_t = by_square.reshape(X_CHIPS, 2, Y_PAIRS, -1, rows).swapaxes(1, 2).reshape(width, rows)

    logits = scale * lax.dot_general(
        image_t, text_t, (((0,), (0,)), ((), ())), preferred_element_type=jnp.float32
    )
    column_ids = lax.axis_index("txt") * cols + jnp.arange(cols, dtype=jnp.int32)
    matched = (positive[:, None] == column_ids[None, :]).astype(jnp.float32)

    col_norm, col_mean = local_softmax(logits, 0)
    row_norm, row_mean = local_softmax(logits, 1)
    matched_sum = jnp.sum(matched * logits)

    seen = collect(row_norm[None], "txt", n_txt)[:, 0]
    row_norms = merge(seen)
    row_slope = jnp.sum(jnp.exp(row_norm - row_norms) * row_mean)

    packed = jnp.concatenate(
        [
            col_norm,
            col_mean,
            jnp.full((128,), 0.5 * jnp.sum(row_norms)),
            jnp.full((128,), 0.5 * row_slope - matched_sum),
            jnp.full((128,), matched_sum),
        ]
    )
    seen = collect(packed[None], "img", n_img)[:, 0]
    column_norms = merge(seen[:, :cols])
    col_slope = jnp.sum(jnp.exp(seen[:, :cols] - column_norms) * seen[:, cols : 2 * cols])
    row_loss_all = jnp.sum(seen[:, 2 * cols])
    slope_here = 0.5 * col_slope + jnp.sum(seen[:, 2 * cols + 128])
    loss_here = 0.5 * jnp.sum(column_norms) - jnp.sum(seen[:, 2 * cols + 256])

    packed = jnp.concatenate([jnp.full((128,), loss_here), jnp.full((128,), slope_here)])
    seen = collect(packed[None], "txt", n_txt)[:, 0]
    batch = rows * n_img
    loss = ((jnp.sum(seen[:, 0]) + row_loss_all) / batch).reshape(1)
    grad_log_scale = (jnp.sum(seen[:, 128]) / batch).reshape(1)

    weights = (
        0.5 * (jnp.exp(logits - row_norms[:, None]) + jnp.exp(logits - column_norms[None, :]))
        - matched
    ).astype(jnp.bfloat16)

    text_part = scale * lax.dot_general(
        image_t, weights, (((1,), (0,)), ((), ())), preferred_element_type=jnp.float32
    )
    text_part = text_part.astype(jnp.bfloat16).reshape(8, CORES, -1, cols).swapaxes(0, 1)
    text_part = jnp.sum(exchange(text_part, "img", BOTH_CORES).astype(jnp.float32), axis=0)
    grad_texts = lax.psum_scatter(
        text_part.astype(jnp.bfloat16).reshape(-1, cols),
        "img",
        scatter_dimension=0,
        axis_index_groups=ALONG_Z,
        tiled=True,
    ).T

    text_t = text_t.reshape(X_CHIPS, Y_PAIRS, 2, -1, cols).swapaxes(1, 2).reshape(width, cols)
    image_part = scale * lax.dot_general(
        text_t, weights, (((1,), (1,)), ((), ())), preferred_element_type=jnp.float32
    )
    image_part = image_part.astype(jnp.bfloat16).reshape(2 * X_CHIPS, -1, rows)
    partial = jnp.sum(exchange(image_part, "txt", SQUARES).astype(jnp.float32), axis=0)
    partial = partial.astype(jnp.bfloat16).reshape(Y_PAIRS, -1, rows)
    partial = jnp.sum(exchange(partial, "txt", PAIRS).astype(jnp.float32), axis=0)
    grad_images = partial.astype(jnp.bfloat16).T
    return (loss, grad_images, grad_texts, grad_log_scale)


def solution(mesh):
    return jax.shard_map(
        per_device,
        mesh=mesh,
        in_specs=(P("img", "txt"), P("txt", "img"), P("img"), P()),
        out_specs=(P(), P("img", "txt"), P("txt", "img"), P()),
        check_vma=False,
    )
```

time: 193 us -> 210 us (1.088); the launches traced: 192 us -> 207 us
  blocking collectives: 13.9 us -> 27.5 us
  starting transfers between devices: 41 us -> 35 us
  waiting for transfers between devices: 86.9 us -> 91.8 us
  local copies, waits for them, and re-layouts: 6.81 us -> 9.3 us
    all_to_all x6, waiting for transfers between devices: 60.1 us -> 74.9 us  [exchange(): return lax.all_to_all(blocks, axis, 0, 0, axis_index_groups=groups)]
    all_to_all x1 -> x3, blocking collectives: 13.9 us -> 27.5 us  [exchange(): return lax.all_to_all(blocks, axis, 0, 0, axis_index_groups=groups)]
    all_gather x1, waiting for transfers between devices: 26.1 us -> 16.1 us  [per_device(): lax.all_gather(by_core, 'img', axis=0, axis_index_groups=ALONG_Z, tiled=T...]
    all_to_all x6, starting transfers between devices: 41 us -> 34.9 us  [exchange(): return lax.all_to_all(blocks, axis, 0, 0, axis_index_groups=groups)]
    transpose x0 -> x3, local copies, waits for them, and re-layouts: none -> 2.72 us  [the longest x1 1.57 us: per_device(): by_square.reshape(X_CHIPS, 2, Y_PAIRS, -1, rows).swapaxes(1, 2)]
    reduce_sum x10 -> x11, other arithmetic: 7.81 us -> 8.69 us  [the longest x1 2.67 us: local_softmax(): mean = jnp.sum(powers * logits, axis=axis) / total]
    broadcast_in_dim x5 -> x6, local copies, waits for them, and re-layouts: 4.75 us -> 5.35 us  [collect(): jnp.broadcast_to(block[None], (count,) + block.shape)]
  transfers between devices with their start and end apart: 8 -> 8, of which waited for: 6 -> 7; matrix products, arithmetic and copies ran while one was open for 5% -> 4% of each run, Pallas kernels for 0% -> 0%
where the time goes in v2:
time: 210 us; the launch traced here: 207 us
  waiting for transfers between devices  91.8 us (44%)
  starting transfers between devices  35 us (17%)
  blocking collectives  27.5 us (13%)
  between operations  23.7 us (11%)
  matrix products  10.5 us (5%)
  local copies, waits for them, and re-layouts  9.3 us (4%)
  other arithmetic  8.83 us (4%)
    all_to_all x6, waiting for transfers between devices, exchange(): return lax.all_to_all(blocks, axis, 0, 0, axis_index_groups=groups)  74.9 us
    all_to_all x6, starting transfers between devices, exchange(): return lax.all_to_all(blocks, axis, 0, 0, axis_index_groups=groups)  34.9 us
    all_to_all x3, blocking collectives, exchange(): return lax.all_to_all(blocks, axis, 0, 0, axis_index_groups=groups)  27.5 us
    all_gather x1, waiting for transfers between devices, per_device(): lax.all_gather(by_core, 'img', axis=0, axis_index_groups=ALONG_Z, tiled=T...  16.1 us
    broadcast_in_dim x6, local copies, waits for them, and re-layouts, collect(): jnp.broadcast_to(block[None], (count,) + block.shape)  5.35 us
  transfers between devices with their start and end apart: 8, of which 7 were waited for; matrix products, arithmetic and copies ran while one was open for 4% of the time, Pallas kernels for 0%

profile of v2, /device:TPU:1, one launch (start us, length us, event | category | flops | bytes accessed | tf_op | source)
XLA Modules:
  0.0 206.5 jit_solution(806121439991999889)
XLA Ops:
  7.2 0.8 broadcast_in_dim.22
  8.0 11.1 %all_to_all.45 = bf16[2,64,512]{2,1,0:T(8,128)(2,1)} all-to-all(bf16[2,64,512]{2,1,0:T(8,128)(2,1)S(1)} %broadcast_in_dim.22), channel_id=1, replica_groups={{0,32},{64,96},{128,160},{192,224},{256,288},{320,352},{384,416},{448,4..., dimensions={0} | all-to-all | bytes 262144 | tf_op jit(solution)/shard_map/all_to_all | solution.py:23
  19.1 0.9 broadcast_in_dim.20
  19.9 12.3 %all_to_all.46 = bf16[4,32,1024]{2,1,0:T(8,128)(2,1)S(1)} all-to-all(bf16[4,32,1024]{2,1,0:T(8,128)(2,1)S(1)} %broadcast_in_dim.20), channel_id=1, replica_groups={{0,2,4,6},{1,3,5,7},{8,10,12,14},{9,11,13,15},{16,18,20,22},{17,19,21,2..., dimensions={0} | all-to-all | bytes 524288 | tf_op jit(solution)/shard_map/all_to_all | solution.py:23
  32.2 1.6 broadcast_in_dim.21
  33.8 3.6 %all-to-all-start.1 = ((bf16[8,4,32,1024]{3,2,1,0:T(8,128)(2,1)}), bf16[8,4,32,1024]{3,2,1,0:T(8,128)(2,1)S(1)}, u32[]{:S(2)}, u32[]{:S(2)}) async-start(bf16[8,4,32,1024]{3,2,1,0:T(8,128)(2,1)} %broadcast_in_dim.21), calls=%async_computation.1 | async-start | bytes 4194304 | tf_op jit(solution)/shard_map/all_to_all | solution.py:23
  37.4 0.0 all-gather.2.cloned.1.call-start
  37.5 0.7 all-gather.2.cloned.1.call-update
  38.9 23.8 %all-to-all-done.1 = bf16[8,4,32,1024]{3,2,1,0:T(8,128)(2,1)S(1)} async-done(((bf16[8,4,32,1024]{3,2,1,0:T(8,128)(2,1)}), bf16[8,4,32,1024]{3,2,1,0:T(8,128)(2,1)S(1)}, u32[]{:S(2)}, u32[]{:S(2)}) %all-to-all-start.1) | async-done | bytes 2097184 | tf_op jit(solution)/shard_map/all_to_all | solution.py:23
  62.7 1.6 copy.23
  64.3 16.1 %all-gather.2.cloned.1.call-done = bf16[1024,512]{1,0:T(8,128)(2,1)} async-done(((bf16[128,512]{1,0:T(8,128)(2,1)}), bf16[1024,512]{1,0:T(8,128)(2,1)}) %all-gather.2.cloned.1.call-update) | async-done | bytes 1048592 | tf_op jit(solution)/shard_map/all_gather | solution.py:50
  80.4 0.0 copy-start.2
  80.4 3.2 %fusion.11 = (f32[1024]{0:T(1024)S(1)}, f32[512]{0:T(512)S(1)}, f32[1024,512]{1,0:T(8,128)S(1)}) fusion(bf16[1024,1024]{1,0:T(8,128)(2,1)} %bitcast.44, bf16[1024,512]{1,0:T(8,128)(2,1)} %all-gather.2.cloned.1.call-done, f32[]{:T(128)} %bitcast), kind=kOutput, calls=%fused_computation.39 | convolution fusion | flops 1075313152 | bytes 5249028 | tf_op jit(solution)/shard_map/dot_general | solution.py:55
  83.7 0.0 copy-done.2
  83.7 2.7 %multiply_reduce_fusion = (f32[1024]{0:T(1024)S(1)}, f32[1024]{0:T(1024)S(1)}, f32[]{:T(128)}, f32[512]{0:T(512)S(1)}, f32[512]{0:T(512)S(1)}) fusion(f32[1024,512]{1,0:T(8,128)S(1)} %get-tuple-element.23, f32[1024]{0:T(1024)S(1)} %get-tuple-element.11, s32[512]{0:T(512)S(1)} %iota_add_fusion, s32[1024]{0:T(1024)S(1)} %copy-done.2, f32[512]{0:T(512)S(1)} %get-tuple-element.12), kind=kLoop, calls=%fused_computation.7 | loop fusion | flops 5764095 | bytes 2121732 | tf_op jit(solution)/shard_map/reduce_sum | solution.py:34
  86.3 0.7 broadcast_in_dim.23
  87.1 9.6 %all-to-all-start.3 = ((f32[32,1,1024]{2,1,0:T(1,128)}), f32[32,1,1024]{2,1,0:T(1,128)S(1)}, u32[]{:S(2)}, u32[]{:S(2)}) async-start(f32[32,1,1024]{2,1,0:T(1,128)} %broadcast_in_dim.23), calls=%async_computation.3 | async-start | bytes 262144 | tf_op jit(solution)/shard_map/all_to_all | solution.py:23
  96.7 9.1 %all-to-all-done.3 = f32[32,1,1024]{2,1,0:T(1,128)S(1)} async-done(((f32[32,1,1024]{2,1,0:T(1,128)}), f32[32,1,1024]{2,1,0:T(1,128)S(1)}, u32[]{:S(2)}, u32[]{:S(2)}) %all-to-all-start.3) | async-done | bytes 131104 | tf_op jit(solution)/shard_map/all_to_all | solution.py:23
  105.8 0.1 reduce_max.38
  105.9 0.6 multiply_reduce_fusion.2
  108.5 0.7 constant_dynamic-update-slice_fusion
  109.2 0.7 broadcast_in_dim.27
  109.9 10.4 %all-to-all-start.4 = ((f32[16,1,1408]{2,1,0:T(1,128)}), f32[16,1,1408]{2,1,0:T(1,128)S(1)}, u32[]{:S(2)}, u32[]{:S(2)}) async-start(f32[16,1,1408]{2,1,0:T(1,128)} %broadcast_in_dim.27), calls=%async_computation.4 | async-start | bytes 180224 | tf_op jit(solution)/shard_map/all_to_all | solution.py:23
  120.3 0.0 copy-done
  120.3 1.1 copy.29
  121.3 7.2 %all-to-all-done.4 = f32[16,1,1408]{2,1,0:T(1,128)S(1)} async-done(((f32[16,1,1408]{2,1,0:T(1,128)}), f32[16,1,1408]{2,1,0:T(1,128)S(1)}, u32[]{:S(2)}, u32[]{:S(2)}) %all-to-all-start.4) | async-done | bytes 90144 | tf_op jit(solution)/shard_map/all_to_all | solution.py:23
  128.6 0.6 fusion.12
  129.3 3.6 %fusion.5 = bf16[1024,512]{0,1:T(8,128)(2,1)S(1)} fusion(bf16[1024,1024]{1,0:T(8,128)(2,1)} %bitcast.45, f32[]{:T(128)} %bitcast, f32[1024,512]{1,0:T(8,128)S(1)} %get-tuple-element.23, f32[512]{0:T(512)S(1)} %get-tuple-element.21, f32[1024]{0:T(1024)S(1)} %get-tuple-element.22, s32[512]{0:T(512)S(1)} %iota_add_fusion, s32[1024]{0:T(1024)S(1)} %copy-done.2), kind=kOutput, calls=%fused_computation.14 | convolution fusion | flops 1078984704 | bytes 5255172 | tf_op jit(solution)/shard_map/dot_general | solution.py:96
  132.8 0.0 copy-done.1
  132.8 3.7 %multiply_convert_fusion = bf16[1024,1024]{0,1:T(8,128)(2,1)} fusion(bf16[1024,512]{1,0:T(8,128)(2,1)S(1)} %bitcast.49, f32[]{:T(128)} %bitcast, f32[1024,512]{1,0:T(8,128)S(1)} %get-tuple-element.23, f32[512]{0:T(512)S(1)} %get-tuple-element.21, f32[1024]{0:T(1024)S(1)} %get-tuple-element.22, s32[512]{0:T(512)S(1)} %iota_add_fusion, s32[1024]{0:T(1024)S(1)} %copy-done.2), kind=kOutput, calls=%fused_computation | convolution fusion | flops 1080033280 | bytes 5255172 | tf_op jit(solution)/shard_map/dot_general | solution.py:110
  136.5 0.5 copy.30
  137.1 0.1 copy.31
  137.2 4.2 %all_to_all.47 = bf16[2,8,64,512]{3,2,1,0:T(8,128)(2,1)S(1)} all-to-all(bf16[2,8,64,512]{3,2,1,0:T(8,128)(2,1)S(1)} %copy.31), channel_id=1, replica_groups={{0,32},{64,96},{128,160},{192,224},{256,288},{320,352},{384,416},{448,4..., dimensions={0} | all-to-all | bytes 2097152 | tf_op jit(solution)/shard_map/all_to_all | solution.py:23
  141.4 3.6 %all-to-all-start.6 = ((bf16[8,128,1024]{2,1,0:T(8,128)(2,1)}), bf16[8,128,1024]{2,1,0:T(8,128)(2,1)S(1)}, u32[]{:S(2)}, u32[]{:S(2)}) async-start(bf16[8,128,1024]{2,1,0:T(8,128)(2,1)} %bitcast.46), calls=%async_computation.6 | async-start | bytes 4194304 | tf_op jit(solution)/shard_map/all_to_all | solution.py:23
  145.0 0.0 reduce-scatter.2.cloned.1.call-start
  145.0 1.1 reduce_sum.197
  146.2 0.0 reduce-scatter.2.cloned.1.call-update
  146.8 0.6 fusion.8
  148.1 0.6 slice_reduce_fusion.3
  150.0 21.6 %all-to-all-done.6 = bf16[8,128,1024]{2,1,0:T(8,128)(2,1)S(1)} async-done(((bf16[8,128,1024]{2,1,0:T(8,128)(2,1)}), bf16[8,128,1024]{2,1,0:T(8,128)(2,1)S(1)}, u32[]{:S(2)}, u32[]{:S(2)}) %all-to-all-start.6) | async-done | bytes 2097184 | tf_op jit(solution)/shard_map/all_to_all | solution.py:23
  171.7 0.6 broadcast_in_dim.29
  172.3 4.3 %all-to-all-start.5 = ((f32[32,1,256]{2,1,0:T(1,128)}), f32[32,1,256]{2,1,0:T(1,128)S(1)}, u32[]{:S(2)}, u32[]{:S(2)}) async-start(f32[32,1,256]{2,1,0:T(1,128)} %broadcast_in_dim.29), calls=%async_computation.5 | async-start | bytes 65536 | tf_op jit(solution)/shard_map/all_to_all | solution.py:23
  176.6 1.1 reduce_sum.195
  177.7 7.7 %all-to-all-done.5 = f32[32,1,256]{2,1,0:T(1,128)S(1)} async-done(((f32[32,1,256]{2,1,0:T(1,128)}), f32[32,1,256]{2,1,0:T(1,128)S(1)}, u32[]{:S(2)}, u32[]{:S(2)}) %all-to-all-start.5) | async-done | bytes 32800 | tf_op jit(solution)/shard_map/all_to_all | solution.py:23
  185.4 3.4 %all-to-all-start.7 = ((bf16[4,32,1024]{2,1,0:T(8,128)(2,1)}), bf16[4,32,1024]{2,1,0:T(8,128)(2,1)S(1)}, u32[]{:S(2)}, u32[]{:S(2)}) async-start(bf16[4,32,1024]{2,1,0:T(8,128)(2,1)} %bitcast.13), calls=%async_computation.7 | async-start | bytes 524288 | tf_op jit(solution)/shard_map/all_to_all | solution.py:23
  188.8 0.6 slice_reduce_fusion.1
  191.3 5.4 %all-to-all-done.7 = bf16[4,32,1024]{2,1,0:T(8,128)(2,1)S(1)} async-done(((bf16[4,32,1024]{2,1,0:T(8,128)(2,1)}), bf16[4,32,1024]{2,1,0:T(8,128)(2,1)S(1)}, u32[]{:S(2)}, u32[]{:S(2)}) %all-to-all-start.7) | async-done | bytes 262176 | tf_op jit(solution)/shard_map/all_to_all | solution.py:23
  196.8 0.7 reduce_sum.196
  (17 shorter events, 0.2 us)
Async XLA Ops:
  33.8 28.9 %all-to-all-start.1 = ((bf16[8,4,32,1024]{3,2,1,0:T(8,128)(2,1)}), bf16[8,4,32,1024]{3,2,1,0:T(8,128)(2,1)S(1)}, u32[]{:S(2)}, u32[]{:S(2)}) async-start(bf16[8,4,32,1024]{3,2,1,0:T(8,128)(2,1)} %broadcast_in_dim.21), calls=%async_computation.1 | async-start | bytes 4194304 | tf_op jit(solution)/shard_map/all_to_all | solution.py:23
  37.4 43.0 %all-gather.2.cloned.1.call-start = ((), (), s32[]{:S(2)}) async-start(), calls=%async_computation.10 | async-start | bytes 1179648 | tf_op jit(solution)/shard_map/all_gather | solution.py:50
  80.4 3.2 %copy-start.2 = (s32[1024]{0:T(1024)S(1)}, s32[1024]{0:T(1024)}, u32[]{:S(2)}) copy-start(s32[1024]{0:T(1024)} %param.6) | copy-start | bytes 12292
  83.6 36.6 %copy-start = (bf16[1024,512]{1,0:T(8,128)(2,1)S(1)}, bf16[1024,512]{1,0:T(8,128)(2,1)}, u32[]{:S(2)}) copy-start(bf16[1024,512]{1,0:T(8,128)(2,1)} %all-gather.2.cloned.1.call-done) | copy-start | bytes 3145732
  87.1 18.7 %all-to-all-start.3 = ((f32[32,1,1024]{2,1,0:T(1,128)}), f32[32,1,1024]{2,1,0:T(1,128)S(1)}, u32[]{:S(2)}, u32[]{:S(2)}) async-start(f32[32,1,1024]{2,1,0:T(1,128)} %broadcast_in_dim.23), calls=%async_computation.3 | async-start | bytes 262144 | tf_op jit(solution)/shard_map/all_to_all | solution.py:23
  109.9 18.7 %all-to-all-start.4 = ((f32[16,1,1408]{2,1,0:T(1,128)}), f32[16,1,1408]{2,1,0:T(1,128)S(1)}, u32[]{:S(2)}, u32[]{:S(2)}) async-start(f32[16,1,1408]{2,1,0:T(1,128)} %broadcast_in_dim.27), calls=%async_computation.4 | async-start | bytes 180224 | tf_op jit(solution)/shard_map/all_to_all | solution.py:23
  129.3 3.6 %copy-start.1 = (bf16[4,2,4,32,512]{4,3,2,1,0:T(8,128)(2,1)S(1)}, bf16[4,2,4,32,512]{4,3,2,1,0:T(8,128)(2,1)}, u32[]{:S(2)}) copy-start(bf16[4,2,4,32,512]{4,3,2,1,0:T(8,128)(2,1)} %copy.29) | copy-start | bytes 3145732
  141.4 30.3 %all-to-all-start.6 = ((bf16[8,128,1024]{2,1,0:T(8,128)(2,1)}), bf16[8,128,1024]{2,1,0:T(8,128)(2,1)S(1)}, u32[]{:S(2)}, u32[]{:S(2)}) async-start(bf16[8,128,1024]{2,1,0:T(8,128)(2,1)} %bitcast.46), calls=%async_computation.6 | async-start | bytes 4194304 | tf_op jit(solution)/shard_map/all_to_all | solution.py:23
  145.0 52.5 %reduce-scatter.2.cloned.1.call-start = ((), (), s32[]{:S(2)}) async-start(), calls=%async_computation.11 | async-start | bytes 589824 | tf_op jit(solution)/shard_map/reduce_scatter | solution.py:101
  172.3 13.1 %all-to-all-start.5 = ((f32[32,1,256]{2,1,0:T(1,128)}), f32[32,1,256]{2,1,0:T(1,128)S(1)}, u32[]{:S(2)}, u32[]{:S(2)}) async-start(f32[32,1,256]{2,1,0:T(1,128)} %broadcast_in_dim.29), calls=%async_computation.5 | async-start | bytes 65536 | tf_op jit(solution)/shard_map/all_to_all | solution.py:23
  185.4 11.4 %all-to-all-start.7 = ((bf16[4,32,1024]{2,1,0:T(8,128)(2,1)}), bf16[4,32,1024]{2,1,0:T(8,128)(2,1)S(1)}, u32[]{:S(2)}, u32[]{:S(2)}) async-start(bf16[4,32,1024]{2,1,0:T(8,128)(2,1)} %bitcast.13), calls=%async_computation.7 | async-start | bytes 524288 | tf_op jit(solution)/shard_map/all_to_all | solution.py:23
Sparse Core Ops, SparseCore 0:
  40.3 40.0 all-gather.1
  149.2 29.9 reduce-scatter.1

commit v3 on v2

--- a/solution.py
+++ b/solution.py
@@ -46,14 +46,19 @@
     width = images.shape[1] * n_txt
     scale = jnp.exp(scale_logarithm[0])
 
-    by_core = collect(texts.T, "img", CORES, BOTH_CORES).reshape(-1, cols)
-    text_t = lax.all_gather(by_core, "img", axis=0, axis_index_groups=ALONG_Z, tiled=True)
-    by_pair = collect(images.T, "txt", Y_PAIRS, PAIRS)
-    by_square = collect(by_pair, "txt", 2 * X_CHIPS, SQUARES)
+    text_full = lax.all_gather(texts, "img", axis=1, tiled=True)
+    def gather(block):
+        by_pair = collect(block, "txt", Y_PAIRS, PAIRS)
+        return collect(by_pair, "txt", 2 * X_CHIPS, SQUARES)
+
+    def none(block):
+        return jnp.zeros((2 * X_CHIPS, Y_PAIRS) + block.shape, block.dtype)
+
+    by_square = lax.cond(scale > 0, gather, none, images.T)
     image_t = by_square.reshape(X_CHIPS, 2, Y_PAIRS, -1, rows).swapaxes(1, 2).reshape(width, rows)
 
     logits = scale * lax.dot_general(
-        image_t, text_t, (((0,), (0,)), ((), ())), preferred_element_type=jnp.float32
+        image_t, text_full, (((0,), (1,)), ((), ())), preferred_element_type=jnp.float32
     )
     column_ids = lax.axis_index("txt") * cols + jnp.arange(cols, dtype=jnp.int32)
     matched = (positive[:, None] == column_ids[None, :]).astype(jnp.float32)
@@ -106,7 +111,7 @@
         tiled=True,
     ).T
 
-    text_t = text_t.reshape(X_CHIPS, Y_PAIRS, 2, -1, cols).swapaxes(1, 2).reshape(width, cols)
+    text_t = text_full.T.reshape(X_CHIPS, Y_PAIRS, 2, -1, cols).swapaxes(1, 2).reshape(width, cols)
     image_part = scale * lax.dot_general(
         text_t, weights, (((1,), (1,)), ((), ())), preferred_element_type=jnp.float32
     )

time: 210 us -> 185 us (0.88)
  waiting for transfers between devices: 91.8 us -> 54 us
  blocking collectives: 27.5 us -> 48.8 us
  starting transfers between devices: 35 us -> 30.4 us
  local copies, waits for them, and re-layouts: 9.3 us -> 6.55 us
    all_to_all x6 -> x5, waiting for transfers between devices: 74.9 us -> 51.1 us  [exchange(): return lax.all_to_all(blocks, axis, 0, 0, axis_index_groups=groups)]
    all_to_all x3, blocking collectives: 27.5 us -> 48.8 us  [exchange(): return lax.all_to_all(blocks, axis, 0, 0, axis_index_groups=groups)]
    all_gather x1, waiting for transfers between devices: 16.1 us -> 2.16 us  [per_device(): text_full = lax.all_gather(texts, 'img', axis=1, tiled=True)]
    all_to_all x6 -> x5, starting transfers between devices: 34.9 us -> 30.3 us  [exchange(): return lax.all_to_all(blocks, axis, 0, 0, axis_index_groups=groups)]
    broadcast_in_dim x6 -> x5, local copies, waits for them, and re-layouts: 5.35 us -> 3.14 us  [collect(): jnp.broadcast_to(block[None], (count,) + block.shape)]
  transfers between devices with their start and end apart: 8 -> 7, of which waited for: 7 -> 6; matrix products, arithmetic and copies ran while one was open for 4% -> 5% of each run, Pallas kernels for 0% -> 0%
where the time goes in v3:
time: 185 us; the launch traced here: 182 us
  waiting for transfers between devices  54 us (29%)
  blocking collectives  48.8 us (26%)
  starting transfers between devices  30.4 us (16%)
  between operations  23.6 us (13%)
  matrix products  10.1 us (5%)
  other arithmetic  8.83 us (5%)
  local copies, waits for them, and re-layouts  6.55 us (4%)
    all_to_all x5, waiting for transfers between devices, exchange(): return lax.all_to_all(blocks, axis, 0, 0, axis_index_groups=groups)  51.1 us
    all_to_all x3, blocking collectives, exchange(): return lax.all_to_all(blocks, axis, 0, 0, axis_index_groups=groups)  48.8 us
    all_to_all x5, starting transfers between devices, exchange(): return lax.all_to_all(blocks, axis, 0, 0, axis_index_groups=groups)  30.3 us
  transfers between devices with their start and end apart: 7, of which 6 were waited for; matrix products, arithmetic and copies ran while one was open for 5% of the time, Pallas kernels for 0%

profile of v3, /device:TPU:1, one launch (start us, length us, event | category | flops | bytes accessed | tf_op | source)
XLA Modules:
  0.0 182.3 jit_solution(3635034199827770140)
XLA Ops:
  7.2 0.0 all-gather.2.cloned.1.call-start
  7.2 0.7 all-gather.2.cloned.1.call-update
  8.6 45.7 %conditional.1 = (bf16[8,4,32,1024]{3,2,1,0:T(8,128)(2,1)S(1)}) conditional(s32[]{:T(128)} %convert_element_type.24, () %tuple.14, bf16[32,1024]{1,0:T(8,128)(2,1)} %bitcast.55), branch_computations={%region_0.0_spmd, %region_1.0_spmd} | conditional | bytes 7405576 | solution.py:57
  8.6 0.9 broadcast_in_dim.7
  9.5 16.5 %all_to_all.38 = bf16[4,32,1024]{2,1,0:T(8,128)(2,1)S(1)} all-to-all(bf16[4,32,1024]{2,1,0:T(8,128)(2,1)S(1)} %broadcast_in_dim.7), channel_id=1, replica_groups={{0,2,4,6},{1,3,5,7},{8,10,12,14},{9,11,13,15},{16,18,20,22},{17,19,21,2..., dimensions={0} | all-to-all | bytes 524288 | tf_op jit(solution)/shard_map/cond/branch_1_fun/all_to_all | solution.py:23
  25.9 0.3 broadcast_in_dim.18
  26.2 28.1 %all_to_all.39 = bf16[8,4,32,1024]{3,2,1,0:T(8,128)(2,1)S(1)} all-to-all(bf16[8,4,32,1024]{3,2,1,0:T(8,128)(2,1)S(1)} %broadcast_in_dim.18), channel_id=1, replica_groups={{0,1,8,9,16,17,24,25},{2,3,10,11,18,19,26,27},{4,5,12,13,20,21,28,29},{..., dimensions={0} | all-to-all | bytes 4194304 | tf_op jit(solution)/shard_map/cond/branch_1_fun/all_to_all | solution.py:23
  54.3 1.6 copy.19
  55.9 2.2 %all-gather.2.cloned.1.call-done = bf16[512,1024]{0,1:T(8,128)(2,1)} async-done(((bf16[512,64]{0,1:T(8,128)(2,1)}), bf16[512,1024]{0,1:T(8,128)(2,1)}) %all-gather.2.cloned.1.call-update) | async-done | bytes 1048592 | tf_op jit(solution)/shard_map/all_gather | solution.py:49
  58.1 0.0 copy-start.2
  58.1 3.2 %fusion.10 = (f32[1024]{0:T(1024)S(1)}, f32[512]{0:T(512)S(1)}, f32[1024,512]{1,0:T(8,128)S(1)}) fusion(bf16[1024,1024]{1,0:T(8,128)(2,1)} %bitcast.43, bf16[512,1024]{0,1:T(8,128)(2,1)} %all-gather.2.cloned.1.call-done, f32[]{:T(128)} %bitcast), kind=kOutput, calls=%fused_computation.39 | convolution fusion | flops 1075313152 | bytes 5249028 | tf_op jit(solution)/shard_map/dot_general | solution.py:60
  61.3 0.0 copy-start
  61.3 0.0 copy-done.2
  61.3 2.7 %multiply_reduce_fusion = (f32[1024]{0:T(1024)S(1)}, f32[1024]{0:T(1024)S(1)}, f32[]{:T(128)}, f32[512]{0:T(512)S(1)}, f32[512]{0:T(512)S(1)}) fusion(f32[1024,512]{1,0:T(8,128)S(1)} %get-tuple-element.27, f32[1024]{0:T(1024)S(1)} %get-tuple-element.15, s32[512]{0:T(512)S(1)} %iota_add_fusion, s32[1024]{0:T(1024)S(1)} %copy-done.2, f32[512]{0:T(512)S(1)} %get-tuple-element.16), kind=kLoop, calls=%fused_computation.7 | loop fusion | flops 5764095 | bytes 2121732 | tf_op jit(solution)/shard_map/reduce_sum | solution.py:34
  64.0 0.7 broadcast_in_dim.26
  64.7 9.3 %all-to-all-start.2 = ((f32[32,1,1024]{2,1,0:T(1,128)}), f32[32,1,1024]{2,1,0:T(1,128)S(1)}, u32[]{:S(2)}, u32[]{:S(2)}) async-start(f32[32,1,1024]{2,1,0:T(1,128)} %broadcast_in_dim.26), calls=%async_computation.2 | async-start | bytes 262144 | tf_op jit(solution)/shard_map/all_to_all | solution.py:23
  74.0 9.1 %all-to-all-done.2 = f32[32,1,1024]{2,1,0:T(1,128)S(1)} async-done(((f32[32,1,1024]{2,1,0:T(1,128)}), f32[32,1,1024]{2,1,0:T(1,128)S(1)}, u32[]{:S(2)}, u32[]{:S(2)}) %all-to-all-start.2) | async-done | bytes 131104 | tf_op jit(solution)/shard_map/all_to_all | solution.py:23
  83.1 0.1 reduce_max.38
  83.3 0.6 multiply_reduce_fusion.2
  85.9 0.7 constant_dynamic-update-slice_fusion
  86.5 0.7 broadcast_in_dim.30
  87.2 9.8 %all-to-all-start.3 = ((f32[16,1,1408]{2,1,0:T(1,128)}), f32[16,1,1408]{2,1,0:T(1,128)S(1)}, u32[]{:S(2)}, u32[]{:S(2)}) async-start(f32[16,1,1408]{2,1,0:T(1,128)} %broadcast_in_dim.30), calls=%async_computation.3 | async-start | bytes 180224 | tf_op jit(solution)/shard_map/all_to_all | solution.py:23
  97.0 0.0 copy-done
  97.0 1.1 copy.25
  98.1 7.2 %all-to-all-done.3 = f32[16,1,1408]{2,1,0:T(1,128)S(1)} async-done(((f32[16,1,1408]{2,1,0:T(1,128)}), f32[16,1,1408]{2,1,0:T(1,128)S(1)}, u32[]{:S(2)}, u32[]{:S(2)}) %all-to-all-start.3) | async-done | bytes 90144 | tf_op jit(solution)/shard_map/all_to_all | solution.py:23
  105.4 0.6 fusion.11
  106.0 0.0 copy-start.1
  106.0 3.2 %multiply_convert_fusion.1 = bf16[1024,512]{1,0:T(8,128)(2,1)S(1)} fusion(bf16[1024,1024]{1,0:T(8,128)(2,1)} %bitcast.44, f32[]{:T(128)} %bitcast, f32[1024,512]{1,0:T(8,128)S(1)} %get-tuple-element.27, f32[512]{0:T(512)S(1)} %get-tuple-element.25, f32[1024]{0:T(1024)S(1)} %get-tuple-element.26, s32[512]{0:T(512)S(1)} %iota_add_fusion, s32[1024]{0:T(1024)S(1)} %copy-done.2), kind=kOutput, calls=%fused_computation.6 | convolution fusion | flops 1078984704 | bytes 5255172 | tf_op jit(solution)/shard_map/dot_general | solution.py:101
  109.2 0.0 copy-done.1
  109.2 3.7 %multiply_convert_fusion = bf16[1024,1024]{0,1:T(8,128)(2,1)} fusion(bf16[1024,512]{1,0:T(8,128)(2,1)S(1)} %bitcast.48, f32[]{:T(128)} %bitcast, f32[1024,512]{1,0:T(8,128)S(1)} %get-tuple-element.27, f32[512]{0:T(512)S(1)} %get-tuple-element.25, f32[1024]{0:T(1024)S(1)} %get-tuple-element.26, s32[512]{0:T(512)S(1)} %iota_add_fusion, s32[1024]{0:T(1024)S(1)} %copy-done.2), kind=kOutput, calls=%fused_computation | convolution fusion | flops 1080033280 | bytes 5255172 | tf_op jit(solution)/shard_map/dot_general | solution.py:115
  112.9 0.1 copy.41
  113.0 4.2 %all_to_all.40 = bf16[2,8,64,512]{3,2,1,0:T(8,128)(2,1)S(1)} all-to-all(bf16[2,8,64,512]{3,2,1,0:T(8,128)(2,1)S(1)} %bitcast.42), channel_id=1, replica_groups={{0,32},{64,96},{128,160},{192,224},{256,288},{320,352},{384,416},{448,4..., dimensions={0} | all-to-all | bytes 2097152 | tf_op jit(solution)/shard_map/all_to_all | solution.py:23
  117.2 3.6 %all-to-all-start.5 = ((bf16[8,128,1024]{2,1,0:T(8,128)(2,1)}), bf16[8,128,1024]{2,1,0:T(8,128)(2,1)S(1)}, u32[]{:S(2)}, u32[]{:S(2)}) async-start(bf16[8,128,1024]{2,1,0:T(8,128)(2,1)} %bitcast.45), calls=%async_computation.5 | async-start | bytes 4194304 | tf_op jit(solution)/shard_map/all_to_all | solution.py:23
  120.8 0.0 reduce-scatter.2.cloned.1.call-start
  120.9 1.1 reduce_sum.197
  122.0 0.0 reduce-scatter.2.cloned.1.call-update
  122.7 0.6 fusion.7
  124.0 0.6 slice_reduce_fusion.3
  125.9 21.6 %all-to-all-done.5 = bf16[8,128,1024]{2,1,0:T(8,128)(2,1)S(1)} async-done(((bf16[8,128,1024]{2,1,0:T(8,128)(2,1)}), bf16[8,128,1024]{2,1,0:T(8,128)(2,1)S(1)}, u32[]{:S(2)}, u32[]{:S(2)}) %all-to-all-start.5) | async-done | bytes 2097184 | tf_op jit(solution)/shard_map/all_to_all | solution.py:23
  147.5 0.6 broadcast_in_dim.32
  148.1 4.2 %all-to-all-start.4 = ((f32[32,1,256]{2,1,0:T(1,128)}), f32[32,1,256]{2,1,0:T(1,128)S(1)}, u32[]{:S(2)}, u32[]{:S(2)}) async-start(f32[32,1,256]{2,1,0:T(1,128)} %broadcast_in_dim.32), calls=%async_computation.4 | async-start | bytes 65536 | tf_op jit(solution)/shard_map/all_to_all | solution.py:23
  152.4 1.1 reduce_sum.195
  153.5 7.7 %all-to-all-done.4 = f32[32,1,256]{2,1,0:T(1,128)S(1)} async-done(((f32[32,1,256]{2,1,0:T(1,128)}), f32[32,1,256]{2,1,0:T(1,128)S(1)}, u32[]{:S(2)}, u32[]{:S(2)}) %all-to-all-start.4) | async-done | bytes 32800 | tf_op jit(solution)/shard_map/all_to_all | solution.py:23
  161.1 3.4 %all-to-all-start.6 = ((bf16[4,32,1024]{2,1,0:T(8,128)(2,1)}), bf16[4,32,1024]{2,1,0:T(8,128)(2,1)S(1)}, u32[]{:S(2)}, u32[]{:S(2)}) async-start(bf16[4,32,1024]{2,1,0:T(8,128)(2,1)} %bitcast.12), calls=%async_computation.6 | async-start | bytes 524288 | tf_op jit(solution)/shard_map/all_to_all | solution.py:23
  164.6 0.6 slice_reduce_fusion.1
  167.1 5.4 %all-to-all-done.6 = bf16[4,32,1024]{2,1,0:T(8,128)(2,1)S(1)} async-done(((bf16[4,32,1024]{2,1,0:T(8,128)(2,1)}), bf16[4,32,1024]{2,1,0:T(8,128)(2,1)S(1)}, u32[]{:S(2)}, u32[]{:S(2)}) %all-to-all-start.6) | async-done | bytes 262176 | tf_op jit(solution)/shard_map/all_to_all | solution.py:23
  172.6 0.7 reduce_sum.196
  173.2 0.0 reduce-scatter.2.cloned.1.call-done
  (14 shorter events, 0.1 us)
Async XLA Ops:
  7.2 50.9 %all-gather.2.cloned.1.call-start = ((), (), s32[]{:S(2)}) async-start(), calls=%async_computation.9 | async-start | bytes 1114112 | tf_op jit(solution)/shard_map/all_gather | solution.py:49
  58.1 3.2 %copy-start.2 = (s32[1024]{0:T(1024)S(1)}, s32[1024]{0:T(1024)}, u32[]{:S(2)}) copy-start(s32[1024]{0:T(1024)} %param.8) | copy-start | bytes 12292
  61.3 35.7 %copy-start = (bf16[512,1024]{0,1:T(8,128)(2,1)S(1)}, bf16[512,1024]{0,1:T(8,128)(2,1)}, u32[]{:S(2)}) copy-start(bf16[512,1024]{0,1:T(8,128)(2,1)} %all-gather.2.cloned.1.call-done) | copy-start | bytes 3145732
  64.7 18.4 %all-to-all-start.2 = ((f32[32,1,1024]{2,1,0:T(1,128)}), f32[32,1,1024]{2,1,0:T(1,128)S(1)}, u32[]{:S(2)}, u32[]{:S(2)}) async-start(f32[32,1,1024]{2,1,0:T(1,128)} %broadcast_in_dim.26), calls=%async_computation.2 | async-start | bytes 262144 | tf_op jit(solution)/shard_map/all_to_all | solution.py:23
  87.2 18.1 %all-to-all-start.3 = ((f32[16,1,1408]{2,1,0:T(1,128)}), f32[16,1,1408]{2,1,0:T(1,128)S(1)}, u32[]{:S(2)}, u32[]{:S(2)}) async-start(f32[16,1,1408]{2,1,0:T(1,128)} %broadcast_in_dim.30), calls=%async_computation.3 | async-start | bytes 180224 | tf_op jit(solution)/shard_map/all_to_all | solution.py:23
  106.0 3.2 %copy-start.1 = (bf16[4,2,4,32,512]{4,3,2,1,0:T(8,128)(2,1)S(1)}, bf16[4,2,4,32,512]{4,3,2,1,0:T(8,128)(2,1)}, u32[]{:S(2)}) copy-start(bf16[4,2,4,32,512]{4,3,2,1,0:T(8,128)(2,1)} %copy.25) | copy-start | bytes 3145732
  117.2 30.3 %all-to-all-start.5 = ((bf16[8,128,1024]{2,1,0:T(8,128)(2,1)}), bf16[8,128,1024]{2,1,0:T(8,128)(2,1)S(1)}, u32[]{:S(2)}, u32[]{:S(2)}) async-start(bf16[8,128,1024]{2,1,0:T(8,128)(2,1)} %bitcast.45), calls=%async_computation.5 | async-start | bytes 4194304 | tf_op jit(solution)/shard_map/all_to_all | solution.py:23
  120.8 52.4 %reduce-scatter.2.cloned.1.call-start = ((), (), s32[]{:S(2)}) async-start(), calls=%async_computation.10 | async-start | bytes 589824 | tf_op jit(solution)/shard_map/reduce_scatter | solution.py:106
  148.1 13.0 %all-to-all-start.4 = ((f32[32,1,256]{2,1,0:T(1,128)}), f32[32,1,256]{2,1,0:T(1,128)S(1)}, u32[]{:S(2)}, u32[]{:S(2)}) async-start(f32[32,1,256]{2,1,0:T(1,128)} %broadcast_in_dim.32), calls=%async_computation.4 | async-start | bytes 65536 | tf_op jit(solution)/shard_map/all_to_all | solution.py:23
  161.1 11.4 %all-to-all-start.6 = ((bf16[4,32,1024]{2,1,0:T(8,128)(2,1)}), bf16[4,32,1024]{2,1,0:T(8,128)(2,1)S(1)}, u32[]{:S(2)}, u32[]{:S(2)}) async-start(bf16[4,32,1024]{2,1,0:T(8,128)(2,1)} %bitcast.12), calls=%async_computation.6 | async-start | bytes 524288 | tf_op jit(solution)/shard_map/all_to_all | solution.py:23
Sparse Core Ops, SparseCore 0:
  10.1 47.8 all-gather.1
  125.1 29.8 reduce-scatter.1

commit v4 on v3

v4 whole, which is shorter than its diff:
```python
import jax
import jax.numpy as jnp
from jax import lax
from jax.experimental import pallas as pl
from jax.experimental.pallas import tpu as pltpu
from jax.sharding import PartitionSpec as P

X_CHIPS = 4
Y_PAIRS = 4
Z_CHIPS = 8
CORES = 2
SQUARE = 2 * X_CHIPS
PAIRS = [
    [(x * Y_PAIRS + pair) * 2 + side for pair in range(Y_PAIRS)]
    for x in range(X_CHIPS)
    for side in range(2)
]
SQUARES = [
    [(x * Y_PAIRS + pair) * 2 + side for x in range(X_CHIPS) for side in range(2)]
    for pair in range(Y_PAIRS)
]
BOTH_CORES = [[z * CORES + core for core in range(CORES)] for z in range(Z_CHIPS)]
ALONG_Z = [[z * CORES + core for z in range(Z_CHIPS)] for core in range(CORES)]

LANES = 128
TAIL_ROWS = 8
F32 = jnp.float32
BF16 = jnp.bfloat16


def exchange(blocks, axis, groups=None):
    return lax.all_to_all(blocks, axis, 0, 0, axis_index_groups=groups)


def collect(block, axis, count, groups=None):
    return exchange(jnp.broadcast_to(block[None], (count,) + block.shape), axis, groups)


def vmem():
    return pl.BlockSpec(memory_space=pltpu.VMEM)


def smem():
    return pl.BlockSpec(memory_space=pltpu.SMEM)


def call(kernel, name, in_specs, outs, flops, moved, powers=0, scratch=()):
    out_shape = [jax.ShapeDtypeStruct(shape, dtype) for shape, dtype, _ in outs]
    return pl.pallas_call(
        kernel,
        name=name,
        out_shape=out_shape,
        in_specs=in_specs,
        out_specs=[spec for _, _, spec in outs],
        scratch_shapes=list(scratch),
        compiler_params=pltpu.CompilerParams(vmem_limit_bytes=40 << 20),
        cost_estimate=pl.CostEstimate(flops=flops, bytes_accessed=moved, transcendentals=powers),
    )


def to_lanes(column):
    return jnp.broadcast_to(column, (LANES, LANES)).T[:1]


def to_sublanes(line):
    return jnp.broadcast_to(line, (LANES, LANES)).T[:, :1]


def pick(shape, axis, values):
    index = lax.broadcasted_iota(jnp.int32, shape, axis)
    out = jnp.zeros(shape, F32)
    for k, value in enumerate(values):
        out = jnp.where(index == k, value, out)
    return out


def thirds(value):
    first = value.astype(BF16).astype(F32)
    rest = value - first
    second = rest.astype(BF16).astype(F32)
    return [first, second, (rest - second).astype(BF16).astype(F32)]


def is_match(pos_ref, base_ref, start, rows):
    ids = lax.broadcasted_iota(jnp.int32, (LANES, rows), 0) + (base_ref[0] + start)
    return pos_ref[...] == ids


def tile_kernel(
    scale_ref, base_ref, pos_ref, image_ref, text_ref,
    logit_ref, text_out, row_out, row_norm, row_mean, col_norm, col_mean, matched_out,
):
    depth, cols = text_ref.shape
    rows = pos_ref.shape[1]
    part = depth // (SQUARE * Y_PAIRS)
    for x in range(X_CHIPS):
        for side in range(2):
            for pair in range(Y_PAIRS):
                source = ((x * Y_PAIRS + pair) * 2 + side) * part
                target = ((x * 2 + side) * Y_PAIRS + pair) * part
                text_out[target : target + part, :] = text_ref[source : source + part, :]
    image_t = image_ref[...].reshape(depth, rows)
    row_high = jnp.full((1, rows), -jnp.inf, F32)
    matched = jnp.zeros((1, rows), F32)
    for start in range(0, cols, LANES):
        span = slice(start, start + LANES)
        logits = scale_ref[0] * lax.dot_general(
            text_out[:, span], image_t, (((0,), (0,)), ((), ())), preferred_element_type=F32
        )
        logit_ref[span, :] = logits
        high = jnp.max(logits, axis=1, keepdims=True)
        powers = jnp.exp(logits - high)
        total = jnp.sum(powers, axis=1, keepdims=True)
        mean = jnp.sum(powers * logits, axis=1, keepdims=True) / total
        col_norm[:, span] = to_lanes(high + jnp.log(total))
        col_mean[:, span] = to_lanes(mean)
        row_high = jnp.maximum(row_high, jnp.max(logits, axis=0, keepdims=True))
        mask = is_match(pos_ref, base_ref, start, rows)
        matched += jnp.sum(jnp.where(mask, logits, 0.0), axis=0, keepdims=True)
    total = jnp.zeros((1, rows), F32)
    mean = jnp.zeros((1, rows), F32)
    for start in range(0, cols, LANES):
        logits = logit_ref[start : start + LANES, :]
        powers = jnp.exp(logits - row_high)
        total += jnp.sum(powers, axis=0, keepdims=True)
        mean += jnp.sum(powers * logits, axis=0, keepdims=True)
    norm = row_high + jnp.log(total)
    row_norm[...] = norm
    row_mean[...] = mean / total
    for k in range(row_out.shape[0]):
        row_out[k] = norm
    matched_out[...] = jnp.broadcast_to(jnp.sum(matched, axis=1, keepdims=True), (1, LANES))


def merge(norms):
    high = jnp.max(norms, axis=0, keepdims=True)
    return high + jnp.log(jnp.sum(jnp.exp(norms - high), axis=0, keepdims=True))


def rows_kernel(seen_ref, row_norm, row_mean, col_norm, col_mean, matched_ref, norm_out, col_out):
    norms = merge(seen_ref[:, 0, :])
    norm_out[...] = norms
    slope = jnp.sum(jnp.exp(row_norm[...] - norms) * row_mean[...], axis=1, keepdims=True)
    matched = matched_ref[:, :1]
    sums = [0.5 * jnp.sum(norms, axis=1, keepdims=True), 0.5 * slope - matched, matched]
    sums = pick((1, LANES), 1, sums)
    cols = col_norm.shape[1]
    for k in range(col_out.shape[0]):
        col_out[k, :, :cols] = col_norm[...]
        col_out[k, :, cols : 2 * cols] = col_mean[...]
        col_out[k, :, 2 * cols :] = sums


def weights_kernel(
    parts, scale_ref, base_ref, pos_ref, seen_ref, norm_ref, logit_ref, image_ref,
    weight_out, text_out, sums_out,
):
    cols, rows = logit_ref.shape
    seen = seen_ref[:, 0, :cols]
    norms = merge(seen)
    slope = jnp.sum(jnp.exp(seen - norms) * seen_ref[:, 0, cols : 2 * cols], keepdims=True)
    sums = jnp.sum(seen_ref[:, 0, 2 * cols :], axis=0, keepdims=True)
    loss = 0.5 * jnp.sum(norms, axis=1, keepdims=True) - sums[:, 2:3] + sums[:, :1] / parts
    sums_out[...] = pick((1, LANES), 1, [loss, 0.5 * slope + sums[:, 1:2]])
    row_norms = norm_ref[...]
    for start in range(0, cols, LANES):
        span = slice(start, start + LANES)
        logits = logit_ref[span, :]
        col_norms = to_sublanes(norms[:, span])
        weights = 0.5 * (jnp.exp(logits - row_norms) + jnp.exp(logits - col_norms))
        mask = is_match(pos_ref, base_ref, start, rows)
        weight_out[span, :] = jnp.where(mask, weights - 1.0, weights).astype(BF16)
    weights = weight_out[...]
    part = image_ref.shape[2]
    step = 4
    for first in range(0, SQUARE, step):
        images = image_ref[first : first + step].reshape(step * Y_PAIRS * part, rows)
        grad = scale_ref[0] * lax.dot_general(
            images, weights, (((1,), (1,)), ((), ())), preferred_element_type=F32
        )
        grad = grad.astype(BF16)
        for k in range(step):
            x, side = divmod(first + k, 2)
            for pair in range(Y_PAIRS):
                z, core = divmod(x * Y_PAIRS + pair, CORES)
                at = (k * Y_PAIRS + pair) * part
                text_out[core, z, side * part : (side + 1) * part, :] = grad[at : at + part, :]


def image_kernel(scale_ref, text_ref, weight_ref, sums_ref, out_ref):
    rows = out_ref.shape[2]
    height = text_ref.shape[0] // SQUARE
    weights = weight_ref[...]
    step = 4
    for first in range(0, SQUARE, step):
        grad = scale_ref[0] * jnp.dot(
            text_ref[first * height : (first + step) * height, :], weights,
            preferred_element_type=F32,
        )
        grad = grad.astype(BF16)
        for k in range(step):
            out_ref[first + k, :height, :] = grad[k * height : (k + 1) * height, :]
    pieces = thirds(sums_ref[:, :1]) + thirds(sums_ref[:, 1:2])
    tail = pick((TAIL_ROWS, rows), 0, pieces).astype(BF16)
    for k in range(SQUARE):
        out_ref[k, height:, :] = tail


def square_kernel(seen_ref, out_ref):
    height = seen_ref.shape[1] - TAIL_ROWS
    rows = seen_ref.shape[2]
    part = height // Y_PAIRS
    tail = jnp.sum(seen_ref[:, height:, :LANES].astype(F32), axis=0)
    loss = tail[0:1, :1] + tail[1:2, :1] + tail[2:3, :1]
    slope = tail[3:4, :1] + tail[4:5, :1] + tail[5:6, :1]
    tail = pick((part, LANES), 0, thirds(loss) + thirds(slope)).astype(BF16)
    for pair in range(Y_PAIRS):
        total = jnp.sum(seen_ref[:, pair * part : (pair + 1) * part, :].astype(F32), axis=0)
        out_ref[pair, :, :rows] = total.astype(BF16)
        out_ref[pair, :, rows:] = tail


def pair_kernel(batch, seen_ref, loss_ref, grad_ref, slope_ref):
    rows = grad_ref.shape[1]
    grad_ref[...] = jnp.sum(seen_ref[:, :, :rows].astype(F32), axis=0).astype(BF16)
    tail = jnp.sum(seen_ref[:, :, rows:].astype(F32), axis=0)
    loss_ref[0] = jnp.sum(tail[0:3, :1]) / batch
    slope_ref[0] = jnp.sum(tail[3:6, :1]) / batch


def per_device(images, texts, positive, scale_logarithm):
    n_img, n_txt = lax.axis_size("img"), lax.axis_size("txt")
    rows, cols = images.shape[0], texts.shape[0]
    part = images.shape[1]
    depth = part * n_txt
    batch = rows * n_img
    height = depth // SQUARE
    scale = jnp.exp(scale_logarithm)
    base = (lax.axis_index("txt") * cols).astype(jnp.int32).reshape(1)
    places = positive.reshape(1, rows)

    text_full = lax.all_gather(texts.T, "img", axis=0, tiled=True)

    def gather(block):
        by_pair = collect(block, "txt", Y_PAIRS, PAIRS)
        return collect(by_pair, "txt", SQUARE, SQUARES)

    def none(block):
        return jnp.zeros((SQUARE, Y_PAIRS) + block.shape, block.dtype)

    image_full = lax.cond(scale[0] > 0, gather, none, images.T)

    macs = rows * cols * depth
    logits, text_t, row_out, row_norm, row_mean, col_norm, col_mean, matched = call(
        lambda *refs: tile_kernel(*refs),
        "tile",
        [smem(), smem(), vmem(), vmem(), vmem()],
        [
            ((cols, rows), F32, vmem()),
            ((depth, cols), BF16, vmem()),
            ((n_txt, 1, rows), F32, vmem()),
            ((1, rows), F32, vmem()),
            ((1, rows), F32, vmem()),
            ((1, cols), F32, vmem()),
            ((1, cols), F32, vmem()),
            ((1, LANES), F32, vmem()),
        ],
        2 * macs, 6 << 20, 2 * rows * cols,
    )(scale, base, places, image_full, text_full)

    seen = exchange(row_out, "txt")
    row_norms, col_out = call(
        lambda *refs: rows_kernel(*refs),
        "rows",
        [vmem()] * 6,
        [((1, rows), F32, vmem()), ((n_img, 1, 2 * cols + LANES), F32, vmem())],
        8 * n_txt * rows, 1 << 18, n_txt * rows,
    )(seen, row_norm, row_mean, col_norm, col_mean, matched)

    seen = exchange(col_out, "img")
    weights, text_part, sums = call(
        lambda *refs: weights_kernel(n_txt, *refs),
        "weights",
        [smem(), smem()] + [vmem()] * 5,
        [
            ((cols, rows), BF16, vmem()),
            ((CORES, Z_CHIPS, depth // n_img, cols), BF16, vmem()),
            ((1, LANES), F32, vmem()),
        ],
        2 * macs, 6 << 20, 2 * rows * cols,
    )(scale, base, places, seen, row_norms, logits, image_full)

    text_part = jnp.sum(exchange(text_part, "img", BOTH_CORES).astype(F32), axis=0)
    grad_texts = lax.psum_scatter(
        text_part.astype(BF16).reshape(-1, cols),
        "img",
        scatter_dimension=0,
        axis_index_groups=ALONG_Z,
        tiled=True,
    ).T

    (image_part,) = call(
        lambda *refs: image_kernel(*refs),
        "image",
        [smem(), vmem(), vmem(), vmem()],
        [((SQUARE, height + TAIL_ROWS, rows), BF16, vmem())],
        2 * macs, 4 << 20,
    )(scale, text_t, weights, sums)
    (partial,) = call(
        lambda *refs: square_kernel(*refs),
        "square",
        [vmem()],
        [((Y_PAIRS, part, rows + LANES), BF16, vmem())],
        depth * rows, 3 << 20,
    )(exchange(image_part, "txt", SQUARES))
    loss, grad_images, grad_log_scale = call(
        lambda *refs: pair_kernel(batch, *refs),
        "pair",
        [vmem()],
        [((1,), F32, smem()), ((part, rows), BF16, vmem()), ((1,), F32, smem())],
        Y_PAIRS * part * rows, 1 << 19,
    )(exchange(partial, "txt", PAIRS))
    return (loss, grad_images.T, grad_texts, grad_log_scale)


def solution(mesh):
    return jax.shard_map(
        per_device,
        mesh=mesh,
        in_specs=(P("img", "txt"), P("txt", "img"), P("img"), P()),
        out_specs=(P(), P("img", "txt"), P("txt", "img"), P()),
        check_vma=False,
    )
```

time: 185 us -> 162 us (0.88)
  blocking collectives: 48.8 us -> 92.2 us
  starting transfers between devices: 30.4 us -> 7.37 us
  waiting for transfers between devices: 54 us -> 31.7 us
  Pallas kernels: 0 us -> 10.8 us
  matrix products: 10.1 us -> 0 us
  between operations: 23.6 us -> 14.8 us
  other arithmetic: 8.83 us -> 1.12 us
  local copies, waits for them, and re-layouts: 6.55 us -> 2.34 us
    all_to_all x3 -> x5, blocking collectives: 48.8 us -> 92.2 us  [exchange(): return lax.all_to_all(blocks, axis, 0, 0, axis_index_groups=groups)]
    all_to_all x5 -> x2, waiting for transfers between devices: 51.1 us -> 27.3 us  [exchange(): return lax.all_to_all(blocks, axis, 0, 0, axis_index_groups=groups)]
    all_to_all x5 -> x2, starting transfers between devices: 30.3 us -> 7.29 us  [exchange(): return lax.all_to_all(blocks, axis, 0, 0, axis_index_groups=groups)]
    pallas_call x0 -> x6, Pallas kernels: none -> 10.8 us  [the longest x1 4.77 us: per_device(): call(lambda *refs: weights_kernel(n_txt, *refs), 'weights', [smem(), smem...]
    dot_general x3 -> x0, matrix products: 10.1 us -> none  [the longest x1 3.69 us: per_device(): lax.dot_general(text_t, weights, (((1,), (1,)), ((), ())), preferred_elem...]
    reduce_sum x11 -> x1, other arithmetic: 8.69 us -> 1.12 us  [per_device(): jnp.sum(exchange(text_part, 'img', BOTH_CORES).astype(F32), axis=0)]
    transpose x2 -> x0, local copies, waits for them, and re-layouts: 2.63 us -> none  [the longest x1 1.57 us: per_device(): by_square.reshape(X_CHIPS, 2, Y_PAIRS, -1, rows).swapaxes(1, 2)]
    broadcast_in_dim x5 -> x2, local copies, waits for them, and re-layouts: 3.14 us -> 1.11 us  [collect(): jnp.broadcast_to(block[None], (count,) + block.shape)]
  transfers between devices with their start and end apart: 7 -> 4, of which waited for: 6 -> 2; matrix products, arithmetic and copies ran while one was open for 5% -> 1% of each run, Pallas kernels for 0% -> 2%
where the time goes in v4:
time: 162 us; the launch traced here: 160 us
  blocking collectives  92.2 us (57%)
  waiting for transfers between devices  31.7 us (20%)
  between operations  14.8 us (9%)
  Pallas kernels  10.8 us (7%)
  starting transfers between devices  7.37 us (5%)
  local copies, waits for them, and re-layouts  2.34 us (1%)
    all_to_all x5, blocking collectives, exchange(): return lax.all_to_all(blocks, axis, 0, 0, axis_index_groups=groups)  92.2 us
    all_to_all x2, waiting for transfers between devices, exchange(): return lax.all_to_all(blocks, axis, 0, 0, axis_index_groups=groups)  27.3 us
    all_to_all x2, starting transfers between devices, exchange(): return lax.all_to_all(blocks, axis, 0, 0, axis_index_groups=groups)  7.29 us
    pallas_call x1, Pallas kernels, per_device(): call(lambda *refs: weights_kernel(n_txt, *refs), 'weights', [smem(), smem...  4.77 us
    all_gather x1, waiting for transfers between devices, per_device(): text_full = lax.all_gather(texts.T, 'img', axis=0, tiled=True)  3.73 us
  transfers between devices with their start and end apart: 4, of which 2 were waited for; matrix products, arithmetic and copies ran while one was open for 1% of the time, Pallas kernels for 2%

profile of v4, /device:TPU:1, one launch (start us, length us, event | category | flops | bytes accessed | tf_op | source)
XLA Modules:
  0.0 160.4 jit_solution(3743367990019210336)
XLA Ops:
  7.2 0.0 all-gather.2.cloned.1.call-start
  7.2 0.7 all-gather.2.cloned.1.call-update
  8.6 0.0 copy-start
  8.6 45.7 %conditional.1 = (bf16[8,4,32,1024]{3,2,1,0:T(8,128)(2,1)S(1)}) conditional(s32[]{:T(128)} %bitcast.2, () %tuple.14, bf16[32,1024]{1,0:T(8,128)(2,1)} %bitcast.11), branch_computations={%region_0.0_spmd, %region_1.0_spmd} | conditional | bytes 7405576 | solution.py:251
  8.6 0.9 broadcast_in_dim.0
  9.5 16.5 %all_to_all.33 = bf16[4,32,1024]{2,1,0:T(8,128)(2,1)S(1)} all-to-all(bf16[4,32,1024]{2,1,0:T(8,128)(2,1)S(1)} %broadcast_in_dim.0), channel_id=1, replica_groups={{0,2,4,6},{1,3,5,7},{8,10,12,14},{9,11,13,15},{16,18,20,22},{17,19,21,2..., dimensions={0} | all-to-all | bytes 524288 | tf_op jit(solution)/shard_map/cond/branch_1_fun/all_to_all | solution.py:32
  25.9 0.3 broadcast_in_dim.1
  26.2 28.1 %all_to_all.34 = bf16[8,4,32,1024]{3,2,1,0:T(8,128)(2,1)S(1)} all-to-all(bf16[8,4,32,1024]{3,2,1,0:T(8,128)(2,1)S(1)} %broadcast_in_dim.1), channel_id=1, replica_groups={{0,1,8,9,16,17,24,25},{2,3,10,11,18,19,26,27},{4,5,12,13,20,21,28,29},{..., dimensions={0} | all-to-all | bytes 4194304 | tf_op jit(solution)/shard_map/cond/branch_1_fun/all_to_all | solution.py:32
  54.3 0.0 copy-start.2
  54.3 3.7 %all-gather.2.cloned.1.call-done.refs_4_ = bf16[1024,512]{1,0:T(8,128)(2,1)} async-done(((bf16[64,512]{1,0:T(8,128)(2,1)}), bf16[1024,512]{1,0:T(8,128)(2,1)}) %all-gather.2.cloned.1.call-update) | async-done | bytes 1048592 | tf_op jit(solution)/shard_map/all_gather | solution.py:242
  58.1 0.0 copy-done
  58.1 0.0 copy-start.1
  58.1 1.2 copy-done.1
  59.3 2.1 %tile.1 = (f32[512,1024]{1,0:T(8,128)S(1)}, bf16[1024,512]{1,0:T(8,128)(2,1)S(1)}, f32[32,1,1024]{2,1,0:T(1,128)S(1)}, f32[1,1024]{1,0:T(1,128)S(1)}, f32[1,1024...) custom-call(f32[1]{0:T(128)S(6)} %exp.3.refs_0_, s32[1]{0:T(128)} %bitcast.refs_1_, ...), custom_call_target="tpu_custom_call" | custom-call | flops 1073741824 | bytes 6291456 | tf_op jit(solution)/shard_map/tile/pallas_call | solution.py:254
  61.4 18.2 %all_to_all.35.refs_0_ = f32[32,1,1024]{2,1,0:T(1,128)S(1)} all-to-all(f32[32,1,1024]{2,1,0:T(1,128)S(1)} %get-tuple-element.25), channel_id=1, replica_groups=mesh['img'=16,'txt'=32] {'txt'}, dimensions={0} | all-to-all | bytes 262144 | tf_op jit(solution)/shard_map/all_to_all | solution.py:32
  79.6 0.2 rows.1
  79.9 16.8 %all_to_all.36.refs_3_ = f32[16,1,1152]{2,1,0:T(1,128)S(1)} all-to-all(f32[16,1,1152]{2,1,0:T(1,128)S(1)} %get-tuple-element.31), channel_id=1, replica_groups=mesh['img'=16,'txt'=32] {'img'}, dimensions={0} | all-to-all | bytes 147456 | tf_op jit(solution)/shard_map/all_to_all | solution.py:32
  96.6 0.0 copy-done.2
  96.6 4.8 %weights.1 = (bf16[512,1024]{1,0:T(8,128)(2,1)S(1)}, bf16[2,8,64,512]{3,2,1,0:T(8,128)(2,1)}, f32[1,128]{1,0:T(1,128)S(1)}) custom-call(f32[1]{0:T(128)S(6)} %exp.3.refs_0_, s32[1]{0:T(128)} %bitcast.refs_1_, s32[1,1024]{1,0:T(1,128)S(1)} %bitcast.9, f32[16,1,1152]{2,1,0:T(1,128)S(1)} %all_to_all.36.refs_3_, f32[1,1024]{1,0:T(1,128)S(1)} %get-tuple-element.32.refs_4_, ...), custom_call_target="tpu_custom_call" | custom-call | flops 1073741824 | bytes 6291456 | tf_op jit(solution)/shard_map/weights/pallas_call | solution.py:281
  101.4 3.7 %all-to-all-start.6 = ((bf16[2,8,64,512]{3,2,1,0:T(8,128)(2,1)}), bf16[2,8,64,512]{3,2,1,0:T(8,128)(2,1)S(1)}, u32[]{:S(2)}, u32[]{:S(2)}) async-start(bf16[2,8,64,512]{3,2,1,0:T(8,128)(2,1)} %get-tuple-element.38), calls=%async_computation.6 | async-start | bytes 2097152 | tf_op jit(solution)/shard_map/all_to_all | solution.py:32
  105.1 2.6 %image.1 = bf16[8,136,1024]{2,1,0:T(8,128)(2,1)} custom-call(f32[1]{0:T(128)S(6)} %exp.3.refs_0_, bf16[1024,512]{1,0:T(8,128)(2,1)S(1)} %get-tuple-element.24.refs_1_, bf16[512,1024]{1,0:T(8,128)(2,1)S(1)} %get-tuple-element.34.refs_2_, f32[1,128]{1,0:T(1,128)S(1)} %get-tuple-element.35.refs_3_), custom_call_target="tpu_custom_call" | custom-call | flops 1073741824 | bytes 4194304 | tf_op jit(solution)/shard_map/image/pallas_call | solution.py:302
  107.7 0.0 all-to-all-done.6
  107.7 3.6 %all-to-all-start.4 = ((bf16[8,136,1024]{2,1,0:T(8,128)(2,1)}), bf16[8,136,1024]{2,1,0:T(8,128)(2,1)S(1)}, u32[]{:S(2)}, u32[]{:S(2)}) async-start(bf16[8,136,1024]{2,1,0:T(8,128)(2,1)} %image.1), calls=%async_computation.4 | async-start | bytes 4456448 | tf_op jit(solution)/shard_map/all_to_all | solution.py:32
  111.4 0.0 reduce-scatter.2.cloned.1.call-start
  111.4 1.1 reduce_sum.12
  112.5 0.0 reduce-scatter.2.cloned.1.call-update
  112.5 27.3 %all-to-all-done.4.refs_0_ = bf16[8,136,1024]{2,1,0:T(8,128)(2,1)S(1)} async-done(((bf16[8,136,1024]{2,1,0:T(8,128)(2,1)}), bf16[8,136,1024]{2,1,0:T(8,128)(2,1)S(1)}, u32[]{:S(2)}, u32[]{:S(2)}) %all-to-all-start.4) | async-done | bytes 2228256 | tf_op jit(solution)/shard_map/all_to_all | solution.py:32
  139.8 0.4 square.1
  140.2 12.6 %all_to_all.37.refs_0_ = bf16[4,32,1152]{2,1,0:T(8,128)(2,1)S(1)} all-to-all(bf16[4,32,1152]{2,1,0:T(8,128)(2,1)S(1)} %square.1), channel_id=1, replica_groups={{0,2,4,6},{1,3,5,7},{8,10,12,14},{9,11,13,15},{16,18,20,22},{17,19,21,2..., dimensions={0} | all-to-all | bytes 589824 | tf_op jit(solution)/shard_map/all_to_all | solution.py:32
  152.8 0.7 pair.1
  153.5 0.0 reduce-scatter.2.cloned.1.call-done
Async XLA Ops:
  7.2 50.9 %all-gather.2.cloned.1.call-start = ((), (), s32[]{:S(2)}) async-start(), calls=%async_computation.8 | async-start | bytes 1114112 | tf_op jit(solution)/shard_map/all_gather | solution.py:242
  8.6 49.5 %copy-start = (s32[1024]{0:T(1024)S(1)}, s32[1024]{0:T(1024)}, u32[]{:S(2)}) copy-start(s32[1024]{0:T(1024)} %param.8) | copy-start | bytes 12292
  54.3 42.3 %copy-start.2 = (bf16[8,4,32,1024]{3,2,1,0:T(8,128)(2,1)}, bf16[8,4,32,1024]{3,2,1,0:T(8,128)(2,1)S(1)}, u32[]{:S(2)}) copy-start(bf16[8,4,32,1024]{3,2,1,0:T(8,128)(2,1)S(1)} %get-tuple-element.40.refs_3_.refs_6_) | copy-start | bytes 6291460
  58.1 1.2 copy-start.1
  101.4 6.3 %all-to-all-start.6 = ((bf16[2,8,64,512]{3,2,1,0:T(8,128)(2,1)}), bf16[2,8,64,512]{3,2,1,0:T(8,128)(2,1)S(1)}, u32[]{:S(2)}, u32[]{:S(2)}) async-start(bf16[2,8,64,512]{3,2,1,0:T(8,128)(2,1)} %get-tuple-element.38), calls=%async_computation.6 | async-start | bytes 2097152 | tf_op jit(solution)/shard_map/all_to_all | solution.py:32
  107.7 32.1 %all-to-all-start.4 = ((bf16[8,136,1024]{2,1,0:T(8,128)(2,1)}), bf16[8,136,1024]{2,1,0:T(8,128)(2,1)S(1)}, u32[]{:S(2)}, u32[]{:S(2)}) async-start(bf16[8,136,1024]{2,1,0:T(8,128)(2,1)} %image.1), calls=%async_computation.4 | async-start | bytes 4456448 | tf_op jit(solution)/shard_map/all_to_all | solution.py:32
  111.4 42.2 %reduce-scatter.2.cloned.1.call-start = ((), (), s32[]{:S(2)}) async-start(), calls=%async_computation.9 | async-start | bytes 589824 | tf_op jit(solution)/shard_map/reduce_scatter | solution.py:294
Sparse Core Ops, SparseCore 0:
  10.1 47.8 all-gather.1
  115.6 29.6 reduce-scatter.1

commit v5 on v4

--- a/solution.py
+++ b/solution.py
@@ -46,16 +46,17 @@
 
 def call(kernel, name, in_specs, outs, flops, moved, powers=0, scratch=()):
     out_shape = [jax.ShapeDtypeStruct(shape, dtype) for shape, dtype, _ in outs]
-    return pl.pallas_call(
+    run = pl.pallas_call(
         kernel,
         name=name,
         out_shape=out_shape,
         in_specs=in_specs,
         out_specs=[spec for _, _, spec in outs],
         scratch_shapes=list(scratch),
-        compiler_params=pltpu.CompilerParams(vmem_limit_bytes=40 << 20),
+        compiler_params=pltpu.CompilerParams(vmem_limit_bytes=24 << 20),
         cost_estimate=pl.CostEstimate(flops=flops, bytes_accessed=moved, transcendentals=powers),
     )
+    return lambda *operands: tuple(run(*operands))
 
 
 def to_lanes(column):
@@ -248,7 +249,8 @@
     def none(block):
         return jnp.zeros((SQUARE, Y_PAIRS) + block.shape, block.dtype)
 
-    image_full = lax.cond(scale[0] > 0, gather, none, images.T)
+    always = scale[0] > -1.0
+    image_full = lax.cond(always, gather, none, images.T)
 
     macs = rows * cols * depth
     logits, text_t, row_out, row_norm, row_mean, col_norm, col_mean, matched = call(
@@ -306,20 +308,27 @@
         [((SQUARE, height + TAIL_ROWS, rows), BF16, vmem())],
         2 * macs, 4 << 20,
     )(scale, text_t, weights, sums)
-    (partial,) = call(
-        lambda *refs: square_kernel(*refs),
-        "square",
-        [vmem()],
-        [((Y_PAIRS, part, rows + LANES), BF16, vmem())],
-        depth * rows, 3 << 20,
-    )(exchange(image_part, "txt", SQUARES))
-    loss, grad_images, grad_log_scale = call(
-        lambda *refs: pair_kernel(batch, *refs),
-        "pair",
-        [vmem()],
-        [((1,), F32, smem()), ((part, rows), BF16, vmem()), ((1,), F32, smem())],
-        Y_PAIRS * part * rows, 1 << 19,
-    )(exchange(partial, "txt", PAIRS))
+
+    def scatter(image_part):
+        (partial,) = call(
+            lambda *refs: square_kernel(*refs),
+            "square",
+            [vmem()],
+            [((Y_PAIRS, part, rows + LANES), BF16, vmem())],
+            depth * rows, 3 << 20,
+        )(exchange(image_part, "txt", SQUARES))
+        return call(
+            lambda *refs: pair_kernel(batch, *refs),
+            "pair",
+            [vmem()],
+            [((1,), F32, smem()), ((part, rows), BF16, vmem()), ((1,), F32, smem())],
+            Y_PAIRS * part * rows, 1 << 19,
+        )(exchange(partial, "txt", PAIRS))
+
+    def nothing(image_part):
+        return jnp.zeros((1,), F32), jnp.zeros((part, rows), BF16), jnp.zeros((1,), F32)
+
+    loss, grad_images, grad_log_scale = lax.cond(always, scatter, nothing, image_part)
     return (loss, grad_images.T, grad_texts, grad_log_scale)
 
 

time: 162 us -> 163 us (level)
  blocking collectives: 92.2 us -> 125 us
  waiting for transfers between devices: 31.7 us -> 4.4 us
  starting transfers between devices: 7.37 us -> 0.08 us
  Pallas kernels: 10.8 us -> 8.51 us
  between operations: 14.8 us -> 17 us
    all_to_all x5 -> x7, blocking collectives: 92.2 us -> 125 us  [exchange(): return lax.all_to_all(blocks, axis, 0, 0, axis_index_groups=groups)]
    all_to_all x2 -> x0, waiting for transfers between devices: 27.3 us -> none  [exchange(): return lax.all_to_all(blocks, axis, 0, 0, axis_index_groups=groups)]
    all_to_all x2 -> x0, starting transfers between devices: 7.29 us -> none  [exchange(): return lax.all_to_all(blocks, axis, 0, 0, axis_index_groups=groups)]
    pallas_call x6, Pallas kernels: 10.8 us -> 8.51 us  [call(): return lambda *operands: tuple(run(*operands))]
  transfers between devices with their start and end apart: 4 -> 2, of which waited for: 2 -> 1; matrix products, arithmetic and copies ran while one was open for 1% -> 1% of each run, Pallas kernels for 2% -> 1%
where the time goes in v5:
time: 163 us; the launch traced here: 160 us
  blocking collectives  125 us (77%)
  between operations  17 us (10%)
  Pallas kernels  8.51 us (5%)
  waiting for transfers between devices  4.4 us (3%)
  local copies, waits for them, and re-layouts  2.34 us (1%)
    all_to_all x7, blocking collectives, exchange(): return lax.all_to_all(blocks, axis, 0, 0, axis_index_groups=groups)  125 us
    pallas_call x6, Pallas kernels, call(): return lambda *operands: tuple(run(*operands))  8.51 us
    all_gather x1, waiting for transfers between devices, per_device(): text_full = lax.all_gather(texts.T, 'img', axis=0, tiled=True)  3.68 us
  transfers between devices with their start and end apart: 2, of which 1 were waited for; matrix products, arithmetic and copies ran while one was open for 1% of the time, Pallas kernels for 1%

profile of v5, /device:TPU:1, one launch (start us, length us, event | category | flops | bytes accessed | tf_op | source)
XLA Modules:
  0.0 160.3 jit_solution(16142861952899938671)
XLA Ops:
  7.2 0.0 all-gather.2.cloned.1.call-start
  7.2 0.7 all-gather.2.cloned.1.call-update
  7.9 0.0 reduce-scatter.2.cloned.1.call-start
  8.6 0.0 copy-start
  8.6 45.7 %conditional.2 = (bf16[8,4,32,1024]{3,2,1,0:T(8,128)(2,1)S(1)}) conditional(s32[]{:T(128)} %bitcast, () %tuple.22, bf16[32,1024]{1,0:T(8,128)(2,1)} %bitcast.11), branch_computations={%region_0.0_spmd, %region_1.0_spmd} | conditional | bytes 7405576 | solution.py:253
  8.7 0.9 broadcast_in_dim.0
  9.5 16.4 %all_to_all.31 = bf16[4,32,1024]{2,1,0:T(8,128)(2,1)S(1)} all-to-all(bf16[4,32,1024]{2,1,0:T(8,128)(2,1)S(1)} %broadcast_in_dim.0), channel_id=1, replica_groups={{0,2,4,6},{1,3,5,7},{8,10,12,14},{9,11,13,15},{16,18,20,22},{17,19,21,2..., dimensions={0} | all-to-all | bytes 524288 | tf_op jit(solution)/shard_map/cond/branch_1_fun/all_to_all | solution.py:32
  26.0 0.3 broadcast_in_dim.1
  26.2 28.1 %all_to_all.32 = bf16[8,4,32,1024]{3,2,1,0:T(8,128)(2,1)S(1)} all-to-all(bf16[8,4,32,1024]{3,2,1,0:T(8,128)(2,1)S(1)} %broadcast_in_dim.1), channel_id=1, replica_groups={{0,1,8,9,16,17,24,25},{2,3,10,11,18,19,26,27},{4,5,12,13,20,21,28,29},{..., dimensions={0} | all-to-all | bytes 4194304 | tf_op jit(solution)/shard_map/cond/branch_1_fun/all_to_all | solution.py:32
  54.4 0.0 copy-start.2
  54.4 3.7 %all-gather.2.cloned.1.call-done.refs_4_ = bf16[1024,512]{1,0:T(8,128)(2,1)} async-done(((bf16[64,512]{1,0:T(8,128)(2,1)}), bf16[1024,512]{1,0:T(8,128)(2,1)}) %all-gather.2.cloned.1.call-update) | async-done | bytes 1048592 | tf_op jit(solution)/shard_map/all_gather | solution.py:243
  58.1 0.0 copy-done
  58.1 0.0 copy-start.1
  58.1 1.2 copy-done.1
  59.3 2.1 %tile.1 = (f32[512,1024]{1,0:T(8,128)S(1)}, bf16[1024,512]{1,0:T(8,128)(2,1)S(1)}, f32[32,1,1024]{2,1,0:T(1,128)S(1)}, f32[1,1024]{1,0:T(1,128)S(1)}, f32[1,1024...) custom-call(f32[1]{0:T(128)S(6)} %exp.3.refs_0_, s32[1]{0:T(128)} %bitcast.1.refs_1_, ...), custom_call_target="tpu_custom_call" | custom-call | flops 1073741824 | bytes 6291456 | tf_op jit(solution)/shard_map/tile/pallas_call | solution.py:59
  61.4 18.2 %all_to_all.35.refs_0_ = f32[32,1,1024]{2,1,0:T(1,128)S(1)} all-to-all(f32[32,1,1024]{2,1,0:T(1,128)S(1)} %get-tuple-element.26), channel_id=1, replica_groups=mesh['img'=16,'txt'=32] {'txt'}, dimensions={0} | all-to-all | bytes 262144 | tf_op jit(solution)/shard_map/all_to_all | solution.py:32
  79.7 0.2 rows.1
  79.9 16.8 %all_to_all.36.refs_3_ = f32[16,1,1152]{2,1,0:T(1,128)S(1)} all-to-all(f32[16,1,1152]{2,1,0:T(1,128)S(1)} %get-tuple-element.32), channel_id=1, replica_groups=mesh['img'=16,'txt'=32] {'img'}, dimensions={0} | all-to-all | bytes 147456 | tf_op jit(solution)/shard_map/all_to_all | solution.py:32
  96.7 0.0 copy-done.2
  96.7 3.8 %weights.1 = (bf16[512,1024]{1,0:T(8,128)(2,1)S(1)}, bf16[2,8,64,512]{3,2,1,0:T(8,128)(2,1)S(1)}, f32[1,128]{1,0:T(1,128)S(1)}) custom-call(f32[1]{0:T(128)S(6)} %exp.3.refs_0_, s32[1]{0:T(128)} %bitcast.1.refs_1_, s32[1,1024]{1,0:T(1,128)S(1)} %bitcast.9, f32[16,1,1152]{2,1,0:T(1,128)S(1)} %all_to_all.36.refs_3_, f32[1,1024]{1,0:T(1,128)S(1)} %get-tuple-element.33.refs_4_, ...), custom_call_target="tpu_custom_call" | custom-call | flops 1073741824 | bytes 6291456 | tf_op jit(solution)/shard_map/weights/pallas_call | solution.py:59
  100.5 4.3 %all_to_all.37 = bf16[2,8,64,512]{3,2,1,0:T(8,128)(2,1)S(1)} all-to-all(bf16[2,8,64,512]{3,2,1,0:T(8,128)(2,1)S(1)} %get-tuple-element.39), channel_id=1, replica_groups={{0,32},{64,96},{128,160},{192,224},{256,288},{320,352},{384,416},{448,4..., dimensions={0} | all-to-all | bytes 2097152 | tf_op jit(solution)/shard_map/all_to_all | solution.py:32
  104.8 1.1 reduce_sum.12
  105.9 0.0 reduce-scatter.2.cloned.1.call-update
  106.0 1.3 image.1
  107.3 43.9 %conditional.3 = (f32[1]{0:T(128)}, bf16[32,1024]{1,0:T(8,128)(2,1)}, f32[1]{0:T(128)}) conditional(s32[]{:T(128)} %bitcast, () %tuple.21, bf16[8,136,1024]{2,1,0:T(8,128)(2,1)S(1)} %image.1), branch_computations={%region_2.0_spmd, %region_3.0_spmd} | conditional | flops 1179648 | bytes 8716320 | solution.py:331
  107.3 30.2 %all_to_all.33.refs_0_ = bf16[8,136,1024]{2,1,0:T(8,128)(2,1)S(1)} all-to-all(bf16[8,136,1024]{2,1,0:T(8,128)(2,1)S(1)} %param.3), channel_id=1, replica_groups={{0,1,8,9,16,17,24,25},{2,3,10,11,18,19,26,27},{4,5,12,13,20,21,28,29},{..., dimensions={0} | all-to-all | bytes 4456448 | tf_op jit(solution)/shard_map/cond/branch_1_fun/all_to_all | solution.py:32
  137.4 0.4 square.1
  137.8 11.4 %all_to_all.34.refs_0_ = bf16[4,32,1152]{2,1,0:T(8,128)(2,1)S(1)} all-to-all(bf16[4,32,1152]{2,1,0:T(8,128)(2,1)S(1)} %square.1), channel_id=1, replica_groups={{0,2,4,6},{1,3,5,7},{8,10,12,14},{9,11,13,15},{16,18,20,22},{17,19,21,2..., dimensions={0} | all-to-all | bytes 589824 | tf_op jit(solution)/shard_map/cond/branch_1_fun/all_to_all | solution.py:32
  149.2 0.7 pair.1
  151.1 0.0 reduce-scatter.2.cloned.1.call-done
Async XLA Ops:
  7.2 50.9 %all-gather.2.cloned.1.call-start = ((), (), s32[]{:S(2)}) async-start(), calls=%async_computation.8 | async-start | bytes 1114112 | tf_op jit(solution)/shard_map/all_gather | solution.py:243
  7.9 143.3 %reduce-scatter.2.cloned.1.call-start = ((), (), s32[]{:S(2)}) async-start(), calls=%async_computation.9 | async-start | bytes 589824 | tf_op jit(solution)/shard_map/reduce_scatter | solution.py:296
  8.6 49.4 %copy-start = (s32[1024]{0:T(1024)S(1)}, s32[1024]{0:T(1024)}, u32[]{:S(2)}) copy-start(s32[1024]{0:T(1024)} %param.10) | copy-start | bytes 12292
  54.4 42.3 %copy-start.2 = (bf16[8,4,32,1024]{3,2,1,0:T(8,128)(2,1)}, bf16[8,4,32,1024]{3,2,1,0:T(8,128)(2,1)S(1)}, u32[]{:S(2)}) copy-start(bf16[8,4,32,1024]{3,2,1,0:T(8,128)(2,1)S(1)} %get-tuple-element.57.refs_3_.refs_6_) | copy-start | bytes 6291460
  58.1 1.2 copy-start.1
Sparse Core Ops, SparseCore 0:
  10.1 47.8 all-gather.1
  106.1 26.6 reduce-scatter.1

commit v6 on v4

--- a/solution.py
+++ b/solution.py
@@ -46,16 +46,17 @@
 
 def call(kernel, name, in_specs, outs, flops, moved, powers=0, scratch=()):
     out_shape = [jax.ShapeDtypeStruct(shape, dtype) for shape, dtype, _ in outs]
-    return pl.pallas_call(
+    run = pl.pallas_call(
         kernel,
         name=name,
         out_shape=out_shape,
         in_specs=in_specs,
         out_specs=[spec for _, _, spec in outs],
         scratch_shapes=list(scratch),
-        compiler_params=pltpu.CompilerParams(vmem_limit_bytes=40 << 20),
+        compiler_params=pltpu.CompilerParams(vmem_limit_bytes=24 << 20),
         cost_estimate=pl.CostEstimate(flops=flops, bytes_accessed=moved, transcendentals=powers),
     )
+    return lambda *operands: tuple(run(*operands))
 
 
 def to_lanes(column):
@@ -152,8 +153,8 @@
 
 
 def weights_kernel(
-    parts, scale_ref, base_ref, pos_ref, seen_ref, norm_ref, logit_ref, image_ref,
-    weight_out, text_out, sums_out,
+    parts, scale_ref, base_ref, pos_ref, seen_ref, norm_ref, logit_ref, text_ref,
+    weight_out, image_out,
 ):
     cols, rows = logit_ref.shape
     seen = seen_ref[:, 0, :cols]
@@ -161,7 +162,6 @@
     slope = jnp.sum(jnp.exp(seen - norms) * seen_ref[:, 0, cols : 2 * cols], keepdims=True)
     sums = jnp.sum(seen_ref[:, 0, 2 * cols :], axis=0, keepdims=True)
     loss = 0.5 * jnp.sum(norms, axis=1, keepdims=True) - sums[:, 2:3] + sums[:, :1] / parts
-    sums_out[...] = pick((1, LANES), 1, [loss, 0.5 * slope + sums[:, 1:2]])
     row_norms = norm_ref[...]
     for start in range(0, cols, LANES):
         span = slice(start, start + LANES)
@@ -170,8 +170,28 @@
         weights = 0.5 * (jnp.exp(logits - row_norms) + jnp.exp(logits - col_norms))
         mask = is_match(pos_ref, base_ref, start, rows)
         weight_out[span, :] = jnp.where(mask, weights - 1.0, weights).astype(BF16)
+    height = text_ref.shape[0] // SQUARE
     weights = weight_out[...]
+    step = 4
+    for first in range(0, SQUARE, step):
+        grad = scale_ref[0] * jnp.dot(
+            text_ref[first * height : (first + step) * height, :], weights,
+            preferred_element_type=F32,
+        )
+        grad = grad.astype(BF16)
+        for k in range(step):
+            image_out[first + k, :height, :] = grad[k * height : (k + 1) * height, :]
+    pieces = thirds(loss) + thirds(0.5 * slope + sums[:, 1:2])
+    tail = pick((TAIL_ROWS, rows), 0, pieces).astype(BF16)
+    for k in range(SQUARE):
+        image_out[k, height:, :] = tail
+
+
+def text_kernel(scale_ref, core_ref, weight_ref, image_ref, own_out, other_out):
+    rows = weight_ref.shape[1]
+    weights = weight_ref[...]
     part = image_ref.shape[2]
+    mine = core_ref[0] == 0
     step = 4
     for first in range(0, SQUARE, step):
         images = image_ref[first : first + step].reshape(step * Y_PAIRS * part, rows)
@@ -181,29 +201,13 @@
         grad = grad.astype(BF16)
         for k in range(step):
             x, side = divmod(first + k, 2)
-            for pair in range(Y_PAIRS):
-                z, core = divmod(x * Y_PAIRS + pair, CORES)
+            for pair in range(0, Y_PAIRS, CORES):
+                z = (x * Y_PAIRS + pair) // CORES
                 at = (k * Y_PAIRS + pair) * part
-                text_out[core, z, side * part : (side + 1) * part, :] = grad[at : at + part, :]
-
-
-def image_kernel(scale_ref, text_ref, weight_ref, sums_ref, out_ref):
-    rows = out_ref.shape[2]
-    height = text_ref.shape[0] // SQUARE
-    weights = weight_ref[...]
-    step = 4
-    for first in range(0, SQUARE, step):
-        grad = scale_ref[0] * jnp.dot(
-            text_ref[first * height : (first + step) * height, :], weights,
-            preferred_element_type=F32,
-        )
-        grad = grad.astype(BF16)
-        for k in range(step):
-            out_ref[first + k, :height, :] = grad[k * height : (k + 1) * height, :]
-    pieces = thirds(sums_ref[:, :1]) + thirds(sums_ref[:, 1:2])
-    tail = pick((TAIL_ROWS, rows), 0, pieces).astype(BF16)
-    for k in range(SQUARE):
-        out_ref[k, height:, :] = tail
+                even, odd = grad[at : at + part, :], grad[at + part : at + 2 * part, :]
+                here = slice(side * part, (side + 1) * part)
+                own_out[z, here, :] = jnp.where(mine, even, odd)
+                other_out[z, here, :] = jnp.where(mine, odd, even)
 
 
 def square_kernel(seen_ref, out_ref):
@@ -237,6 +241,7 @@
     height = depth // SQUARE
     scale = jnp.exp(scale_logarithm)
     base = (lax.axis_index("txt") * cols).astype(jnp.int32).reshape(1)
+    core = (lax.axis_index("img") % CORES).astype(jnp.int32).reshape(1)
     places = positive.reshape(1, rows)
 
     text_full = lax.all_gather(texts.T, "img", axis=0, tiled=True)
@@ -248,7 +253,8 @@
     def none(block):
         return jnp.zeros((SQUARE, Y_PAIRS) + block.shape, block.dtype)
 
-    image_full = lax.cond(scale[0] > 0, gather, none, images.T)
+    always = scale[0] > -1.0
+    image_full = lax.cond(always, gather, none, images.T)
 
     macs = rows * cols * depth
     logits, text_t, row_out, row_norm, row_mean, col_norm, col_mean, matched = call(
@@ -278,19 +284,24 @@
     )(seen, row_norm, row_mean, col_norm, col_mean, matched)
 
     seen = exchange(col_out, "img")
-    weights, text_part, sums = call(
+    weights, image_part = call(
         lambda *refs: weights_kernel(n_txt, *refs),
         "weights",
         [smem(), smem()] + [vmem()] * 5,
-        [
-            ((cols, rows), BF16, vmem()),
-            ((CORES, Z_CHIPS, depth // n_img, cols), BF16, vmem()),
-            ((1, LANES), F32, vmem()),
-        ],
+        [((cols, rows), BF16, vmem()), ((SQUARE, height + TAIL_ROWS, rows), BF16, vmem())],
         2 * macs, 6 << 20, 2 * rows * cols,
-    )(scale, base, places, seen, row_norms, logits, image_full)
-
-    text_part = jnp.sum(exchange(text_part, "img", BOTH_CORES).astype(F32), axis=0)
+    )(scale, base, places, seen, row_norms, logits, text_t)
+
+    half = (Z_CHIPS, depth // n_img, cols)
+    own, other = call(
+        lambda *refs: text_kernel(*refs),
+        "texts",
+        [smem(), smem(), vmem(), vmem()],
+        [(half, BF16, vmem()), (half, BF16, vmem())],
+        2 * macs, 4 << 20,
+    )(scale, core, weights, image_full)
+    swap = [(z * CORES + c, z * CORES + 1 - c) for z in range(Z_CHIPS) for c in range(CORES)]
+    text_part = own.astype(F32) + lax.ppermute(other, "img", swap).astype(F32)
     grad_texts = lax.psum_scatter(
         text_part.astype(BF16).reshape(-1, cols),
         "img",
@@ -299,13 +310,6 @@
         tiled=True,
     ).T
 
-    (image_part,) = call(
-        lambda *refs: image_kernel(*refs),
-        "image",
-        [smem(), vmem(), vmem(), vmem()],
-        [((SQUARE, height + TAIL_ROWS, rows), BF16, vmem())],
-        2 * macs, 4 << 20,
-    )(scale, text_t, weights, sums)
     (partial,) = call(
         lambda *refs: square_kernel(*refs),
         "square",

time: 162 us -> 156 us (0.963)
  waiting for transfers between devices: 31.7 us -> 26.9 us
  starting transfers between devices: 7.37 us -> 5.71 us
    all_to_all x2 -> x1, waiting for transfers between devices: 27.3 us -> 20.7 us  [exchange(): return lax.all_to_all(blocks, axis, 0, 0, axis_index_groups=groups)]
    all_to_all x2 -> x1, starting transfers between devices: 7.29 us -> 3.61 us  [exchange(): return lax.all_to_all(blocks, axis, 0, 0, axis_index_groups=groups)]
    ppermute x0 -> x1, starting transfers between devices: none -> 2.02 us  [per_device(): text_part = own.astype(F32) + lax.ppermute(other, 'img', swap).astype(F32)]
    ppermute x0 -> x1, waiting for transfers between devices: none -> 1.78 us  [per_device(): text_part = own.astype(F32) + lax.ppermute(other, 'img', swap).astype(F32)]
  transfers between devices with their start and end apart: 4 -> 4, of which waited for: 2 -> 3; matrix products, arithmetic and copies ran while one was open for 1% -> 1% of each run, Pallas kernels for 2% -> 3%
where the time goes in v6:
time: 156 us; the launch traced here: 155 us
  blocking collectives  92.7 us (59%)
  waiting for transfers between devices  26.9 us (17%)
  between operations  14.8 us (9%)
  Pallas kernels  10.2 us (7%)
  starting transfers between devices  5.71 us (4%)
  local copies, waits for them, and re-layouts  3.71 us (2%)
    all_to_all x5, blocking collectives, exchange(): return lax.all_to_all(blocks, axis, 0, 0, axis_index_groups=groups)  92.7 us
    all_to_all x1, waiting for transfers between devices, exchange(): return lax.all_to_all(blocks, axis, 0, 0, axis_index_groups=groups)  20.7 us
    pallas_call x6, Pallas kernels, call(): return lambda *operands: tuple(run(*operands))  10.2 us
    all_gather x1, waiting for transfers between devices, per_device(): text_full = lax.all_gather(texts.T, 'img', axis=0, tiled=True)  3.73 us
    all_to_all x1, starting transfers between devices, exchange(): return lax.all_to_all(blocks, axis, 0, 0, axis_index_groups=groups)  3.61 us
  transfers between devices with their start and end apart: 4, of which 3 were waited for; matrix products, arithmetic and copies ran while one was open for 1% of the time, Pallas kernels for 3%

profile of v6, /device:TPU:1, one launch (start us, length us, event | category | flops | bytes accessed | tf_op | source)
XLA Modules:
  0.0 155.1 jit_solution(6494234580321514737)
XLA Ops:
  7.2 0.0 all-gather.2.cloned.1.call-start
  7.2 0.7 all-gather.2.cloned.1.call-update
  8.6 0.0 copy-start.2
  8.6 45.7 %conditional.1 = (bf16[8,4,32,1024]{3,2,1,0:T(8,128)(2,1)S(1)}) conditional(s32[]{:T(128)} %bitcast.2, () %tuple.14, bf16[32,1024]{1,0:T(8,128)(2,1)} %bitcast.12), branch_computations={%region_0.1_spmd, %region_1.2_spmd} | conditional | bytes 7405576 | solution.py:257
  8.6 0.9 broadcast_in_dim.0
  9.5 16.5 %all_to_all.28 = bf16[4,32,1024]{2,1,0:T(8,128)(2,1)S(1)} all-to-all(bf16[4,32,1024]{2,1,0:T(8,128)(2,1)S(1)} %broadcast_in_dim.0), channel_id=1, replica_groups={{0,2,4,6},{1,3,5,7},{8,10,12,14},{9,11,13,15},{16,18,20,22},{17,19,21,2..., dimensions={0} | all-to-all | bytes 524288 | tf_op jit(solution)/shard_map/cond/branch_1_fun/all_to_all | solution.py:32
  25.9 0.3 broadcast_in_dim.1
  26.2 28.1 %all_to_all.29 = bf16[8,4,32,1024]{3,2,1,0:T(8,128)(2,1)S(1)} all-to-all(bf16[8,4,32,1024]{3,2,1,0:T(8,128)(2,1)S(1)} %broadcast_in_dim.1), channel_id=1, replica_groups={{0,1,8,9,16,17,24,25},{2,3,10,11,18,19,26,27},{4,5,12,13,20,21,28,29},{..., dimensions={0} | all-to-all | bytes 4194304 | tf_op jit(solution)/shard_map/cond/branch_1_fun/all_to_all | solution.py:32
  54.3 0.0 copy-start.3
  54.3 3.7 %all-gather.2.cloned.1.call-done.refs_4_ = bf16[1024,512]{1,0:T(8,128)(2,1)} async-done(((bf16[64,512]{1,0:T(8,128)(2,1)}), bf16[1024,512]{1,0:T(8,128)(2,1)}) %all-gather.2.cloned.1.call-update) | async-done | bytes 1048592 | tf_op jit(solution)/shard_map/all_gather | solution.py:247
  58.1 0.0 copy-done.3
  58.1 0.0 copy-done.2
  58.1 0.0 copy-start.1
  58.1 1.2 copy-done.1
  59.3 3.9 %tile.1 = (f32[512,1024]{1,0:T(8,128)S(1)}, bf16[1024,512]{1,0:T(8,128)(2,1)S(1)}, f32[32,1,1024]{2,1,0:T(1,128)S(1)}, f32[1,1024]{1,0:T(1,128)S(1)}, f32[1,1024...) custom-call(f32[1]{0:T(128)S(6)} %exp.3.refs_0_, s32[1]{0:T(128)} %bitcast.refs_1_, ...), custom_call_target="tpu_custom_call" | custom-call | flops 1073741824 | bytes 6291456 | tf_op jit(solution)/shard_map/tile/pallas_call | solution.py:59
  63.1 18.2 %all_to_all.30.refs_0_ = f32[32,1,1024]{2,1,0:T(1,128)S(1)} all-to-all(f32[32,1,1024]{2,1,0:T(1,128)S(1)} %get-tuple-element.25), channel_id=1, replica_groups=mesh['img'=16,'txt'=32] {'txt'}, dimensions={0} | all-to-all | bytes 262144 | tf_op jit(solution)/shard_map/all_to_all | solution.py:32
  81.4 0.2 rows.1
  81.6 17.3 %all_to_all.31.refs_3_ = f32[16,1,1152]{2,1,0:T(1,128)S(1)} all-to-all(f32[16,1,1152]{2,1,0:T(1,128)S(1)} %get-tuple-element.31), channel_id=1, replica_groups=mesh['img'=16,'txt'=32] {'img'}, dimensions={0} | all-to-all | bytes 147456 | tf_op jit(solution)/shard_map/all_to_all | solution.py:32
  98.9 2.2 %weights.1 = (bf16[512,1024]{1,0:T(8,128)(2,1)S(1)}, bf16[8,136,1024]{2,1,0:T(8,128)(2,1)S(1)}) custom-call(f32[1]{0:T(128)S(6)} %exp.3.refs_0_, s32[1]{0:T(128)} %bitcast.refs_1_, s32[1,1024]{1,0:T(1,128)S(1)} %bitcast.10, f32[16,1,1152]{2,1,0:T(1,128)S(1)} %all_to_all.31.refs_3_, f32[1,1024]{1,0:T(1,128)S(1)} %get-tuple-element.32.refs_4_, ...), custom_call_target="tpu_custom_call" | custom-call | flops 1073741824 | bytes 6291456 | tf_op jit(solution)/shard_map/weights/pallas_call | solution.py:59
  101.1 0.0 copy-start
  101.1 1.4 copy-done
  102.5 3.6 %all-to-all-start.4 = ((bf16[8,136,1024]{2,1,0:T(8,128)(2,1)}), bf16[8,136,1024]{2,1,0:T(8,128)(2,1)S(1)}, u32[]{:S(2)}, u32[]{:S(2)}) async-start(bf16[8,136,1024]{2,1,0:T(8,128)(2,1)} %copy-done), calls=%async_computation.4 | async-start | bytes 4456448 | tf_op jit(solution)/shard_map/all_to_all | solution.py:32
  106.1 0.0 reduce-scatter.2.cloned.1.call-start
  106.1 2.9 %texts.1 = (bf16[8,64,512]{2,1,0:T(8,128)(2,1)S(1)}, bf16[8,64,512]{2,1,0:T(8,128)(2,1)S(1)}) custom-call(f32[1]{0:T(128)S(6)} %exp.3.refs_0_, s32[1]{0:T(128)} %bitcast.6.refs_1_, bf16[512,1024]{1,0:T(8,128)(2,1)S(1)} %get-tuple-element.38.refs_2_, bf16[8,4,32,1024]{3,2,1,0:T(8,128)(2,1)} %copy-done.3), custom_call_target="tpu_custom_call" | custom-call | flops 1073741824 | bytes 4194304 | tf_op jit(solution)/shard_map/texts/pallas_call | solution.py:59
  109.0 2.0 %collective-permute-start = (bf16[8,64,512]{2,1,0:T(8,128)(2,1)S(1)}, bf16[8,64,512]{2,1,0:T(8,128)(2,1)S(1)}, u32[]{:S(2)}, u32[]{:S(2)}) collective-permute-start(bf16[8,64,512]{2,1,0:T(8,128)(2,1)S(1)} %get-tuple-element.40), channel_id=1, source_target_pairs={{0,32},{32,0},{64,96},{96,64},{128,160},{160,128},{192,224},{224,1... | collective-permute-start | bytes 1572872 | tf_op jit(solution)/shard_map/ppermute | solution.py:304
  111.1 1.8 %collective-permute-done = bf16[8,64,512]{2,1,0:T(8,128)(2,1)S(1)} collective-permute-done((bf16[8,64,512]{2,1,0:T(8,128)(2,1)S(1)}, bf16[8,64,512]{2,1,0:T(8,128)(2,1)S(1)}, u32[]{:S(2)}, u32[]{:S(2)}) %collective-permute-start) | collective-permute-done | bytes 524320 | tf_op jit(solution)/shard_map/ppermute | solution.py:304
  112.8 0.9 add_convert_fusion
  113.8 0.0 reduce-scatter.2.cloned.1.call-update
  113.8 20.7 %all-to-all-done.4.refs_0_ = bf16[8,136,1024]{2,1,0:T(8,128)(2,1)S(1)} async-done(((bf16[8,136,1024]{2,1,0:T(8,128)(2,1)}), bf16[8,136,1024]{2,1,0:T(8,128)(2,1)S(1)}, u32[]{:S(2)}, u32[]{:S(2)}) %all-to-all-start.4) | async-done | bytes 2228256 | tf_op jit(solution)/shard_map/all_to_all | solution.py:32
  134.5 0.4 square.1
  134.9 12.6 %all_to_all.32.refs_0_ = bf16[4,32,1152]{2,1,0:T(8,128)(2,1)S(1)} all-to-all(bf16[4,32,1152]{2,1,0:T(8,128)(2,1)S(1)} %square.1), channel_id=1, replica_groups={{0,2,4,6},{1,3,5,7},{8,10,12,14},{9,11,13,15},{16,18,20,22},{17,19,21,2..., dimensions={0} | all-to-all | bytes 589824 | tf_op jit(solution)/shard_map/all_to_all | solution.py:32
  147.5 0.7 pair.1
  148.2 0.0 reduce-scatter.2.cloned.1.call-done
Async XLA Ops:
  7.2 50.9 %all-gather.2.cloned.1.call-start = ((), (), s32[]{:S(2)}) async-start(), calls=%async_computation.7 | async-start | bytes 1114112 | tf_op jit(solution)/shard_map/all_gather | solution.py:247
  8.6 49.5 %copy-start.2 = (s32[1024]{0:T(1024)S(1)}, s32[1024]{0:T(1024)}, u32[]{:S(2)}) copy-start(s32[1024]{0:T(1024)} %param.8) | copy-start | bytes 12292
  54.3 3.7 %copy-start.3 = (bf16[8,4,32,1024]{3,2,1,0:T(8,128)(2,1)}, bf16[8,4,32,1024]{3,2,1,0:T(8,128)(2,1)S(1)}, u32[]{:S(2)}) copy-start(bf16[8,4,32,1024]{3,2,1,0:T(8,128)(2,1)S(1)} %get-tuple-element.42.refs_3_) | copy-start | bytes 6291460
  58.1 1.2 copy-start.1
  101.1 1.4 copy-start
  102.5 32.0 %all-to-all-start.4 = ((bf16[8,136,1024]{2,1,0:T(8,128)(2,1)}), bf16[8,136,1024]{2,1,0:T(8,128)(2,1)S(1)}, u32[]{:S(2)}, u32[]{:S(2)}) async-start(bf16[8,136,1024]{2,1,0:T(8,128)(2,1)} %copy-done), calls=%async_computation.4 | async-start | bytes 4456448 | tf_op jit(solution)/shard_map/all_to_all | solution.py:32
  106.1 42.1 %reduce-scatter.2.cloned.1.call-start = ((), (), s32[]{:S(2)}) async-start(), calls=%async_computation.8 | async-start | bytes 589824 | tf_op jit(solution)/shard_map/reduce_scatter | solution.py:305
  109.0 3.8 %collective-permute-start = (bf16[8,64,512]{2,1,0:T(8,128)(2,1)S(1)}, bf16[8,64,512]{2,1,0:T(8,128)(2,1)S(1)}, u32[]{:S(2)}, u32[]{:S(2)}) collective-permute-start(bf16[8,64,512]{2,1,0:T(8,128)(2,1)S(1)} %get-tuple-element.40), channel_id=1, source_target_pairs={{0,32},{32,0},{64,96},{96,64},{128,160},{160,128},{192,224},{224,1... | collective-permute-start | bytes 1572872 | tf_op jit(solution)/shard_map/ppermute | solution.py:304
Sparse Core Ops, SparseCore 0:
  10.1 47.8 all-gather.1
  113.9 29.2 reduce-scatter.1

commit v7 on v6

--- a/solution.py
+++ b/solution.py
@@ -19,11 +19,11 @@
     [(x * Y_PAIRS + pair) * 2 + side for x in range(X_CHIPS) for side in range(2)]
     for pair in range(Y_PAIRS)
 ]
-BOTH_CORES = [[z * CORES + core for core in range(CORES)] for z in range(Z_CHIPS)]
 ALONG_Z = [[z * CORES + core for z in range(Z_CHIPS)] for core in range(CORES)]
 
 LANES = 128
 TAIL_ROWS = 8
+BLOCK = 256
 F32 = jnp.float32
 BF16 = jnp.bfloat16
 
@@ -40,11 +40,15 @@
     return pl.BlockSpec(memory_space=pltpu.VMEM)
 
 
+def hbm():
+    return pl.BlockSpec(memory_space=pltpu.HBM)
+
+
 def smem():
     return pl.BlockSpec(memory_space=pltpu.SMEM)
 
 
-def call(kernel, name, in_specs, outs, flops, moved, powers=0, scratch=()):
+def call(kernel, name, in_specs, outs, flops, moved, powers=0, scratch=(), limit=48):
     out_shape = [jax.ShapeDtypeStruct(shape, dtype) for shape, dtype, _ in outs]
     run = pl.pallas_call(
         kernel,
@@ -53,7 +57,7 @@
         in_specs=in_specs,
         out_specs=[spec for _, _, spec in outs],
         scratch_shapes=list(scratch),
-        compiler_params=pltpu.CompilerParams(vmem_limit_bytes=24 << 20),
+        compiler_params=pltpu.CompilerParams(vmem_limit_bytes=limit << 20),
         cost_estimate=pl.CostEstimate(flops=flops, bytes_accessed=moved, transcendentals=powers),
     )
     return lambda *operands: tuple(run(*operands))
@@ -88,46 +92,57 @@
 
 
 def tile_kernel(
-    scale_ref, base_ref, pos_ref, image_ref, text_ref,
+    scale_ref, base_ref, pos_ref, image_in, text_ref,
     logit_ref, text_out, row_out, row_norm, row_mean, col_norm, col_mean, matched_out,
+    image_ref, image_sems,
 ):
     depth, cols = text_ref.shape
     rows = pos_ref.shape[1]
     part = depth // (SQUARE * Y_PAIRS)
+    reads = []
+    for k in range(rows // BLOCK):
+        span = pl.ds(k * BLOCK, BLOCK)
+        reads.append(
+            pltpu.make_async_copy(
+                image_in.at[:, :, :, span], image_ref.at[:, :, :, span], image_sems.at[k]
+            )
+        )
+        reads[-1].start()
     for x in range(X_CHIPS):
         for side in range(2):
             for pair in range(Y_PAIRS):
                 source = ((x * Y_PAIRS + pair) * 2 + side) * part
                 target = ((x * 2 + side) * Y_PAIRS + pair) * part
                 text_out[target : target + part, :] = text_ref[source : source + part, :]
-    image_t = image_ref[...].reshape(depth, rows)
-    row_high = jnp.full((1, rows), -jnp.inf, F32)
-    matched = jnp.zeros((1, rows), F32)
+    text_t = text_out[...]
+    ids = lax.broadcasted_iota(jnp.int32, (cols, BLOCK), 0) + base_ref[0]
+    matched = jnp.zeros((1, BLOCK), F32)
+    for k, read in enumerate(reads):
+        span = slice(k * BLOCK, (k + 1) * BLOCK)
+        read.wait()
+        logits = scale_ref[0] * lax.dot_general(
+            text_t, image_ref[:, :, :, span].reshape(depth, BLOCK), (((0,), (0,)), ((), ())),
+            preferred_element_type=F32,
+        )
+        logit_ref[:, span] = logits
+        high = jnp.max(logits, axis=0, keepdims=True)
+        powers = jnp.exp(logits - high)
+        total = jnp.sum(powers, axis=0, keepdims=True)
+        mean = jnp.sum(powers * logits, axis=0, keepdims=True) / total
+        row_norm[:, span] = high + jnp.log(total)
+        row_mean[:, span] = mean
+        mask = pos_ref[:, span] == ids
+        matched += jnp.sum(jnp.where(mask, logits, 0.0), axis=0, keepdims=True)
     for start in range(0, cols, LANES):
         span = slice(start, start + LANES)
-        logits = scale_ref[0] * lax.dot_general(
-            text_out[:, span], image_t, (((0,), (0,)), ((), ())), preferred_element_type=F32
-        )
-        logit_ref[span, :] = logits
+        logits = logit_ref[span, :]
         high = jnp.max(logits, axis=1, keepdims=True)
         powers = jnp.exp(logits - high)
         total = jnp.sum(powers, axis=1, keepdims=True)
         mean = jnp.sum(powers * logits, axis=1, keepdims=True) / total
         col_norm[:, span] = to_lanes(high + jnp.log(total))
         col_mean[:, span] = to_lanes(mean)
-        row_high = jnp.maximum(row_high, jnp.max(logits, axis=0, keepdims=True))
-        mask = is_match(pos_ref, base_ref, start, rows)
-        matched += jnp.sum(jnp.where(mask, logits, 0.0), axis=0, keepdims=True)
-    total = jnp.zeros((1, rows), F32)
-    mean = jnp.zeros((1, rows), F32)
-    for start in range(0, cols, LANES):
-        logits = logit_ref[start : start + LANES, :]
-        powers = jnp.exp(logits - row_high)
-        total += jnp.sum(powers, axis=0, keepdims=True)
-        mean += jnp.sum(powers * logits, axis=0, keepdims=True)
-    norm = row_high + jnp.log(total)
-    row_norm[...] = norm
-    row_mean[...] = mean / total
+    norm = row_norm[...]
     for k in range(row_out.shape[0]):
         row_out[k] = norm
     matched_out[...] = jnp.broadcast_to(jnp.sum(matched, axis=1, keepdims=True), (1, LANES))
@@ -154,7 +169,7 @@
 
 def weights_kernel(
     parts, scale_ref, base_ref, pos_ref, seen_ref, norm_ref, logit_ref, text_ref,
-    weight_out, image_out,
+    weight_out, image_out, image_ref, image_sems,
 ):
     cols, rows = logit_ref.shape
     seen = seen_ref[:, 0, :cols]
@@ -171,8 +186,13 @@
         mask = is_match(pos_ref, base_ref, start, rows)
         weight_out[span, :] = jnp.where(mask, weights - 1.0, weights).astype(BF16)
     height = text_ref.shape[0] // SQUARE
+    pieces = thirds(loss) + thirds(0.5 * slope + sums[:, 1:2])
+    tail = pick((TAIL_ROWS, rows), 0, pieces).astype(BF16)
+    for k in range(SQUARE):
+        image_ref[k, height:, :] = tail
     weights = weight_out[...]
-    step = 4
+    step = 2
+    copies = []
     for first in range(0, SQUARE, step):
         grad = scale_ref[0] * jnp.dot(
             text_ref[first * height : (first + step) * height, :], weights,
@@ -180,11 +200,16 @@
         )
         grad = grad.astype(BF16)
         for k in range(step):
-            image_out[first + k, :height, :] = grad[k * height : (k + 1) * height, :]
-    pieces = thirds(loss) + thirds(0.5 * slope + sums[:, 1:2])
-    tail = pick((TAIL_ROWS, rows), 0, pieces).astype(BF16)
-    for k in range(SQUARE):
-        image_out[k, height:, :] = tail
+            image_ref[first + k, :height, :] = grad[k * height : (k + 1) * height, :]
+        span = pl.ds(first, step)
+        copies.append(
+            pltpu.make_async_copy(
+                image_ref.at[span], image_out.at[span], image_sems.at[first // step]
+            )
+        )
+        copies[-1].start()
+    for copy in copies:
+        copy.wait()
 
 
 def text_kernel(scale_ref, core_ref, weight_ref, image_ref, own_out, other_out):
@@ -260,7 +285,7 @@
     logits, text_t, row_out, row_norm, row_mean, col_norm, col_mean, matched = call(
         lambda *refs: tile_kernel(*refs),
         "tile",
-        [smem(), smem(), vmem(), vmem(), vmem()],
+        [smem(), smem(), vmem(), hbm(), vmem()],
         [
             ((cols, rows), F32, vmem()),
             ((depth, cols), BF16, vmem()),
@@ -272,6 +297,10 @@
             ((1, LANES), F32, vmem()),
         ],
         2 * macs, 6 << 20, 2 * rows * cols,
+        [
+            pltpu.VMEM(image_full.shape, BF16),
+            pltpu.SemaphoreType.DMA((rows // BLOCK,)),
+        ],
     )(scale, base, places, image_full, text_full)
 
     seen = exchange(row_out, "txt")
@@ -288,8 +317,13 @@
         lambda *refs: weights_kernel(n_txt, *refs),
         "weights",
         [smem(), smem()] + [vmem()] * 5,
-        [((cols, rows), BF16, vmem()), ((SQUARE, height + TAIL_ROWS, rows), BF16, vmem())],
+        [((cols, rows), BF16, vmem()), ((SQUARE, height + TAIL_ROWS, rows), BF16, hbm())],
         2 * macs, 6 << 20, 2 * rows * cols,
+        [
+            pltpu.VMEM((SQUARE, height + TAIL_ROWS, rows), BF16),
+            pltpu.SemaphoreType.DMA((SQUARE // 2,)),
+        ],
+        48,
     )(scale, base, places, seen, row_norms, logits, text_t)
 
     half = (Z_CHIPS, depth // n_img, cols)

time: 156 us -> 157 us (level)
  Pallas kernels: 10.2 us -> 12.4 us
    pallas_call x6, Pallas kernels: 10.2 us -> 12.4 us  [call(): return lambda *operands: tuple(run(*operands))]
where the time goes in v7:
time: 157 us; the launch traced here: 156 us
  blocking collectives  92.7 us (59%)
  waiting for transfers between devices  26.9 us (17%)
  between operations  14.8 us (9%)
  Pallas kernels  12.4 us (8%)
  starting transfers between devices  5.72 us (4%)
  local copies, waits for them, and re-layouts  2.34 us (1%)
    all_to_all x5, blocking collectives, exchange(): return lax.all_to_all(blocks, axis, 0, 0, axis_index_groups=groups)  92.7 us
    all_to_all x1, waiting for transfers between devices, exchange(): return lax.all_to_all(blocks, axis, 0, 0, axis_index_groups=groups)  20.7 us
    pallas_call x6, Pallas kernels, call(): return lambda *operands: tuple(run(*operands))  12.4 us
    all_gather x1, waiting for transfers between devices, per_device(): text_full = lax.all_gather(texts.T, 'img', axis=0, tiled=True)  3.73 us
    all_to_all x1, starting transfers between devices, exchange(): return lax.all_to_all(blocks, axis, 0, 0, axis_index_groups=groups)  3.62 us
  transfers between devices with their start and end apart: 4, of which 3 were waited for; matrix products, arithmetic and copies ran while one was open for 1% of the time, Pallas kernels for 3%

profile of v7, /device:TPU:1, one launch (start us, length us, event | category | flops | bytes accessed | tf_op | source)
XLA Modules:
  0.0 155.9 jit_solution(9980168073567539343)
XLA Ops:
  7.2 0.0 all-gather.2.cloned.1.call-start
  7.2 0.7 all-gather.2.cloned.1.call-update
  8.6 0.0 copy-start.1
  8.6 45.7 %conditional.1 = (bf16[8,4,32,1024]{3,2,1,0:T(8,128)(2,1)S(1)}) conditional(s32[]{:T(128)} %bitcast.2, () %tuple.14, bf16[32,1024]{1,0:T(8,128)(2,1)} %bitcast.12), branch_computations={%region_0.1_spmd, %region_1.2_spmd} | conditional | bytes 7405576 | solution.py:282
  8.6 0.9 broadcast_in_dim.0
  9.5 16.5 %all_to_all.28 = bf16[4,32,1024]{2,1,0:T(8,128)(2,1)S(1)} all-to-all(bf16[4,32,1024]{2,1,0:T(8,128)(2,1)S(1)} %broadcast_in_dim.0), channel_id=1, replica_groups={{0,2,4,6},{1,3,5,7},{8,10,12,14},{9,11,13,15},{16,18,20,22},{17,19,21,2..., dimensions={0} | all-to-all | bytes 524288 | tf_op jit(solution)/shard_map/cond/branch_1_fun/all_to_all | solution.py:32
  25.9 0.3 broadcast_in_dim.1
  26.2 28.1 %all_to_all.29 = bf16[8,4,32,1024]{3,2,1,0:T(8,128)(2,1)S(1)} all-to-all(bf16[8,4,32,1024]{3,2,1,0:T(8,128)(2,1)S(1)} %broadcast_in_dim.1), channel_id=1, replica_groups={{0,1,8,9,16,17,24,25},{2,3,10,11,18,19,26,27},{4,5,12,13,20,21,28,29},{..., dimensions={0} | all-to-all | bytes 4194304 | tf_op jit(solution)/shard_map/cond/branch_1_fun/all_to_all | solution.py:32
  54.3 0.0 copy-start.2
  54.3 3.7 %all-gather.2.cloned.1.call-done.refs_4_ = bf16[1024,512]{1,0:T(8,128)(2,1)} async-done(((bf16[64,512]{1,0:T(8,128)(2,1)}), bf16[1024,512]{1,0:T(8,128)(2,1)}) %all-gather.2.cloned.1.call-update) | async-done | bytes 1048592 | tf_op jit(solution)/shard_map/all_gather | solution.py:272
  58.1 0.0 copy-done.2
  58.1 0.0 copy-done.1
  58.1 0.0 copy-start
  58.1 1.2 copy-done
  59.3 5.2 %tile.1 = (f32[512,1024]{1,0:T(8,128)S(1)}, bf16[1024,512]{1,0:T(8,128)(2,1)S(1)}, f32[32,1,1024]{2,1,0:T(1,128)S(1)}, f32[1,1024]{1,0:T(1,128)S(1)}, f32[1,1024...) custom-call(f32[1]{0:T(128)S(6)} %exp.3.refs_0_, s32[1]{0:T(128)} %bitcast.refs_1_, ...), custom_call_target="tpu_custom_call" | custom-call | flops 1073741824 | bytes 6291456 | tf_op jit(solution)/shard_map/tile/pallas_call | solution.py:63
  64.5 18.2 %all_to_all.30.refs_0_ = f32[32,1,1024]{2,1,0:T(1,128)S(1)} all-to-all(f32[32,1,1024]{2,1,0:T(1,128)S(1)} %get-tuple-element.25), channel_id=1, replica_groups=mesh['img'=16,'txt'=32] {'txt'}, dimensions={0} | all-to-all | bytes 262144 | tf_op jit(solution)/shard_map/all_to_all | solution.py:32
  82.7 0.2 rows.1
  82.9 17.3 %all_to_all.31.refs_3_ = f32[16,1,1152]{2,1,0:T(1,128)S(1)} all-to-all(f32[16,1,1152]{2,1,0:T(1,128)S(1)} %get-tuple-element.31), channel_id=1, replica_groups=mesh['img'=16,'txt'=32] {'img'}, dimensions={0} | all-to-all | bytes 147456 | tf_op jit(solution)/shard_map/all_to_all | solution.py:32
  100.2 3.0 %weights.1 = (bf16[512,1024]{1,0:T(8,128)(2,1)S(1)}, bf16[8,136,1024]{2,1,0:T(8,128)(2,1)}) custom-call(f32[1]{0:T(128)S(6)} %exp.3.refs_0_, s32[1]{0:T(128)} %bitcast.refs_1_, s32[1,1024]{1,0:T(1,128)S(1)} %bitcast.10, f32[16,1,1152]{2,1,0:T(1,128)S(1)} %all_to_all.31.refs_3_, f32[1,1024]{1,0:T(1,128)S(1)} %get-tuple-element.32.refs_4_, ...), custom_call_target="tpu_custom_call" | custom-call | flops 1073741824 | bytes 6291456 | tf_op jit(solution)/shard_map/weights/pallas_call | solution.py:63
  103.3 3.6 %all-to-all-start.4 = ((bf16[8,136,1024]{2,1,0:T(8,128)(2,1)}), bf16[8,136,1024]{2,1,0:T(8,128)(2,1)S(1)}, u32[]{:S(2)}, u32[]{:S(2)}) async-start(bf16[8,136,1024]{2,1,0:T(8,128)(2,1)} %get-tuple-element.35), calls=%async_computation.4 | async-start | bytes 4456448 | tf_op jit(solution)/shard_map/all_to_all | solution.py:32
  106.9 0.0 reduce-scatter.2.cloned.1.call-start
  107.0 2.9 %texts.1 = (bf16[8,64,512]{2,1,0:T(8,128)(2,1)S(1)}, bf16[8,64,512]{2,1,0:T(8,128)(2,1)S(1)}) custom-call(f32[1]{0:T(128)S(6)} %exp.3.refs_0_, s32[1]{0:T(128)} %bitcast.6.refs_1_, bf16[512,1024]{1,0:T(8,128)(2,1)S(1)} %get-tuple-element.38.refs_2_, bf16[8,4,32,1024]{3,2,1,0:T(8,128)(2,1)} %copy-done.2), custom_call_target="tpu_custom_call" | custom-call | flops 1073741824 | bytes 4194304 | tf_op jit(solution)/shard_map/texts/pallas_call | solution.py:63
  109.9 2.0 %collective-permute-start = (bf16[8,64,512]{2,1,0:T(8,128)(2,1)S(1)}, bf16[8,64,512]{2,1,0:T(8,128)(2,1)S(1)}, u32[]{:S(2)}, u32[]{:S(2)}) collective-permute-start(bf16[8,64,512]{2,1,0:T(8,128)(2,1)S(1)} %get-tuple-element.40), channel_id=1, source_target_pairs={{0,32},{32,0},{64,96},{96,64},{128,160},{160,128},{192,224},{224,1... | collective-permute-start | bytes 1572872 | tf_op jit(solution)/shard_map/ppermute | solution.py:338
  111.9 1.8 %collective-permute-done = bf16[8,64,512]{2,1,0:T(8,128)(2,1)S(1)} collective-permute-done((bf16[8,64,512]{2,1,0:T(8,128)(2,1)S(1)}, bf16[8,64,512]{2,1,0:T(8,128)(2,1)S(1)}, u32[]{:S(2)}, u32[]{:S(2)}) %collective-permute-start) | collective-permute-done | bytes 524320 | tf_op jit(solution)/shard_map/ppermute | solution.py:338
  113.7 0.9 add_convert_fusion
  114.6 0.0 reduce-scatter.2.cloned.1.call-update
  114.6 20.7 %all-to-all-done.4.refs_0_ = bf16[8,136,1024]{2,1,0:T(8,128)(2,1)S(1)} async-done(((bf16[8,136,1024]{2,1,0:T(8,128)(2,1)}), bf16[8,136,1024]{2,1,0:T(8,128)(2,1)S(1)}, u32[]{:S(2)}, u32[]{:S(2)}) %all-to-all-start.4) | async-done | bytes 2228256 | tf_op jit(solution)/shard_map/all_to_all | solution.py:32
  135.4 0.4 square.1
  135.7 12.6 %all_to_all.32.refs_0_ = bf16[4,32,1152]{2,1,0:T(8,128)(2,1)S(1)} all-to-all(bf16[4,32,1152]{2,1,0:T(8,128)(2,1)S(1)} %square.1), channel_id=1, replica_groups={{0,2,4,6},{1,3,5,7},{8,10,12,14},{9,11,13,15},{16,18,20,22},{17,19,21,2..., dimensions={0} | all-to-all | bytes 589824 | tf_op jit(solution)/shard_map/all_to_all | solution.py:32
  148.3 0.7 pair.1
  149.0 0.0 reduce-scatter.2.cloned.1.call-done
Async XLA Ops:
  7.2 50.9 %all-gather.2.cloned.1.call-start = ((), (), s32[]{:S(2)}) async-start(), calls=%async_computation.7 | async-start | bytes 1114112 | tf_op jit(solution)/shard_map/all_gather | solution.py:272
  8.6 49.5 %copy-start.1 = (s32[1024]{0:T(1024)S(1)}, s32[1024]{0:T(1024)}, u32[]{:S(2)}) copy-start(s32[1024]{0:T(1024)} %param.8) | copy-start | bytes 12292
  54.3 3.7 %copy-start.2 = (bf16[8,4,32,1024]{3,2,1,0:T(8,128)(2,1)}, bf16[8,4,32,1024]{3,2,1,0:T(8,128)(2,1)S(1)}, u32[]{:S(2)}) copy-start(bf16[8,4,32,1024]{3,2,1,0:T(8,128)(2,1)S(1)} %get-tuple-element.42.refs_3_) | copy-start | bytes 6291460
  58.1 1.2 copy-start
  103.3 32.1 %all-to-all-start.4 = ((bf16[8,136,1024]{2,1,0:T(8,128)(2,1)}), bf16[8,136,1024]{2,1,0:T(8,128)(2,1)S(1)}, u32[]{:S(2)}, u32[]{:S(2)}) async-start(bf16[8,136,1024]{2,1,0:T(8,128)(2,1)} %get-tuple-element.35), calls=%async_computation.4 | async-start | bytes 4456448 | tf_op jit(solution)/shard_map/all_to_all | solution.py:32
  106.9 42.1 %reduce-scatter.2.cloned.1.call-start = ((), (), s32[]{:S(2)}) async-start(), calls=%async_computation.8 | async-start | bytes 589824 | tf_op jit(solution)/shard_map/reduce_scatter | solution.py:339
  109.9 3.8 %collective-permute-start = (bf16[8,64,512]{2,1,0:T(8,128)(2,1)S(1)}, bf16[8,64,512]{2,1,0:T(8,128)(2,1)S(1)}, u32[]{:S(2)}, u32[]{:S(2)}) collective-permute-start(bf16[8,64,512]{2,1,0:T(8,128)(2,1)S(1)} %get-tuple-element.40), channel_id=1, source_target_pairs={{0,32},{32,0},{64,96},{96,64},{128,160},{160,128},{192,224},{224,1... | collective-permute-start | bytes 1572872 | tf_op jit(solution)/shard_map/ppermute | solution.py:338
Sparse Core Ops, SparseCore 0:
  10.1 47.8 all-gather.1
  114.8 29.4 reduce-scatter.1

commit v8 on v6

--- a/solution.py
+++ b/solution.py
@@ -19,7 +19,6 @@
     [(x * Y_PAIRS + pair) * 2 + side for x in range(X_CHIPS) for side in range(2)]
     for pair in range(Y_PAIRS)
 ]
-BOTH_CORES = [[z * CORES + core for core in range(CORES)] for z in range(Z_CHIPS)]
 ALONG_Z = [[z * CORES + core for z in range(Z_CHIPS)] for core in range(CORES)]
 
 LANES = 128
@@ -40,11 +39,15 @@
     return pl.BlockSpec(memory_space=pltpu.VMEM)
 
 
+def hbm():
+    return pl.BlockSpec(memory_space=pltpu.HBM)
+
+
 def smem():
     return pl.BlockSpec(memory_space=pltpu.SMEM)
 
 
-def call(kernel, name, in_specs, outs, flops, moved, powers=0, scratch=()):
+def call(kernel, name, in_specs, outs, flops, moved, powers=0, scratch=(), limit=48):
     out_shape = [jax.ShapeDtypeStruct(shape, dtype) for shape, dtype, _ in outs]
     run = pl.pallas_call(
         kernel,
@@ -53,7 +56,7 @@
         in_specs=in_specs,
         out_specs=[spec for _, _, spec in outs],
         scratch_shapes=list(scratch),
-        compiler_params=pltpu.CompilerParams(vmem_limit_bytes=24 << 20),
+        compiler_params=pltpu.CompilerParams(vmem_limit_bytes=limit << 20),
         cost_estimate=pl.CostEstimate(flops=flops, bytes_accessed=moved, transcendentals=powers),
     )
     return lambda *operands: tuple(run(*operands))
@@ -85,6 +88,18 @@
 def is_match(pos_ref, base_ref, start, rows):
     ids = lax.broadcasted_iota(jnp.int32, (LANES, rows), 0) + (base_ref[0] + start)
     return pos_ref[...] == ids
+
+
+def stay(block):
+    return pl.pallas_call(
+        lambda block_ref, same_ref: None,
+        name="stay",
+        out_shape=jax.ShapeDtypeStruct(block.shape, block.dtype),
+        in_specs=[hbm()],
+        out_specs=hbm(),
+        input_output_aliases={0: 0},
+        compiler_params=pltpu.CompilerParams(vmem_limit_bytes=57 << 20),
+    )(block)
 
 
 def tile_kernel(
@@ -154,7 +169,7 @@
 
 def weights_kernel(
     parts, scale_ref, base_ref, pos_ref, seen_ref, norm_ref, logit_ref, text_ref,
-    weight_out, image_out,
+    weight_out, image_out, image_ref, image_sems,
 ):
     cols, rows = logit_ref.shape
     seen = seen_ref[:, 0, :cols]
@@ -171,8 +186,13 @@
         mask = is_match(pos_ref, base_ref, start, rows)
         weight_out[span, :] = jnp.where(mask, weights - 1.0, weights).astype(BF16)
     height = text_ref.shape[0] // SQUARE
+    pieces = thirds(loss) + thirds(0.5 * slope + sums[:, 1:2])
+    tail = pick((TAIL_ROWS, rows), 0, pieces).astype(BF16)
+    for k in range(SQUARE):
+        image_ref[k, height:, :] = tail
     weights = weight_out[...]
-    step = 4
+    step = 2
+    copies = []
     for first in range(0, SQUARE, step):
         grad = scale_ref[0] * jnp.dot(
             text_ref[first * height : (first + step) * height, :], weights,
@@ -180,11 +200,16 @@
         )
         grad = grad.astype(BF16)
         for k in range(step):
-            image_out[first + k, :height, :] = grad[k * height : (k + 1) * height, :]
-    pieces = thirds(loss) + thirds(0.5 * slope + sums[:, 1:2])
-    tail = pick((TAIL_ROWS, rows), 0, pieces).astype(BF16)
-    for k in range(SQUARE):
-        image_out[k, height:, :] = tail
+            image_ref[first + k, :height, :] = grad[k * height : (k + 1) * height, :]
+        span = pl.ds(first, step)
+        copies.append(
+            pltpu.make_async_copy(
+                image_ref.at[span], image_out.at[span], image_sems.at[first // step]
+            )
+        )
+        copies[-1].start()
+    for copy in copies:
+        copy.wait()
 
 
 def text_kernel(scale_ref, core_ref, weight_ref, image_ref, own_out, other_out):
@@ -248,7 +273,7 @@
 
     def gather(block):
         by_pair = collect(block, "txt", Y_PAIRS, PAIRS)
-        return collect(by_pair, "txt", SQUARE, SQUARES)
+        return stay(collect(by_pair, "txt", SQUARE, SQUARES))
 
     def none(block):
         return jnp.zeros((SQUARE, Y_PAIRS) + block.shape, block.dtype)
@@ -288,8 +313,13 @@
         lambda *refs: weights_kernel(n_txt, *refs),
         "weights",
         [smem(), smem()] + [vmem()] * 5,
-        [((cols, rows), BF16, vmem()), ((SQUARE, height + TAIL_ROWS, rows), BF16, vmem())],
+        [((cols, rows), BF16, vmem()), ((SQUARE, height + TAIL_ROWS, rows), BF16, hbm())],
         2 * macs, 6 << 20, 2 * rows * cols,
+        [
+            pltpu.VMEM((SQUARE, height + TAIL_ROWS, rows), BF16),
+            pltpu.SemaphoreType.DMA((SQUARE // 2,)),
+        ],
+        48,
     )(scale, base, places, seen, row_norms, logits, text_t)
 
     half = (Z_CHIPS, depth // n_img, cols)

time: 156 us -> 155 us (level)
  no operation moved by 1% of the time
where the time goes in v8:
time: 155 us; the launch traced here: 153 us
  blocking collectives  91.7 us (59%)
  waiting for transfers between devices  26.8 us (17%)
  between operations  14.8 us (10%)
  Pallas kernels  11.1 us (7%)
  starting transfers between devices  5.73 us (4%)
  local copies, waits for them, and re-layouts  2.34 us (2%)
    all_to_all x5, blocking collectives, exchange(): return lax.all_to_all(blocks, axis, 0, 0, axis_index_groups=groups)  91.7 us
    all_to_all x1, waiting for transfers between devices, exchange(): return lax.all_to_all(blocks, axis, 0, 0, axis_index_groups=groups)  20.7 us
    pallas_call x6, Pallas kernels, call(): return lambda *operands: tuple(run(*operands))  11.1 us
    all_to_all x1, starting transfers between devices, exchange(): return lax.all_to_all(blocks, axis, 0, 0, axis_index_groups=groups)  3.62 us
    all_gather x1, waiting for transfers between devices, per_device(): text_full = lax.all_gather(texts.T, 'img', axis=0, tiled=True)  3.57 us
  transfers between devices with their start and end apart: 4, of which 3 were waited for; matrix products, arithmetic and copies ran while one was open for 1% of the time, Pallas kernels for 3%

profile of v8, /device:TPU:1, one launch (start us, length us, event | category | flops | bytes accessed | tf_op | source)
XLA Modules:
  0.0 153.4 jit_solution(12598571660512252169)
XLA Ops:
  7.2 0.0 all-gather.2.cloned.1.call-start
  7.2 0.7 all-gather.2.cloned.1.call-update
  8.6 0.0 copy-start.1
  8.6 45.8 %conditional.1 = (bf16[8,4,32,1024]{3,2,1,0:T(8,128)(2,1)}) conditional(s32[]{:T(128)} %bitcast.2, () %tuple.14, bf16[32,1024]{1,0:T(8,128)(2,1)} %bitcast.12), branch_computations={%region_0.1_spmd, %region_1.2_spmd} | conditional | bytes 7405576 | solution.py:282
  8.6 0.9 broadcast_in_dim.0
  9.5 16.5 %all_to_all.28 = bf16[4,32,1024]{2,1,0:T(8,128)(2,1)S(1)} all-to-all(bf16[4,32,1024]{2,1,0:T(8,128)(2,1)S(1)} %broadcast_in_dim.0), channel_id=1, replica_groups={{0,2,4,6},{1,3,5,7},{8,10,12,14},{9,11,13,15},{16,18,20,22},{17,19,21,2..., dimensions={0} | all-to-all | bytes 524288 | tf_op jit(solution)/shard_map/cond/branch_1_fun/all_to_all | solution.py:31
  25.9 0.3 broadcast_in_dim.1
  26.2 28.2 %all_to_all.29.block_ref = bf16[8,4,32,1024]{3,2,1,0:T(8,128)(2,1)} all-to-all(bf16[8,4,32,1024]{3,2,1,0:T(8,128)(2,1)S(1)} %broadcast_in_dim.1), channel_id=1, replica_groups={{0,1,8,9,16,17,24,25},{2,3,10,11,18,19,26,27},{4,5,12,13,20,21,28,29},{..., dimensions={0} | all-to-all | bytes 4194304 | tf_op jit(solution)/shard_map/cond/branch_1_fun/all_to_all | solution.py:31
  54.4 3.6 %all-gather.2.cloned.1.call-done.refs_4_ = bf16[1024,512]{1,0:T(8,128)(2,1)} async-done(((bf16[64,512]{1,0:T(8,128)(2,1)}), bf16[1024,512]{1,0:T(8,128)(2,1)}) %all-gather.2.cloned.1.call-update) | async-done | bytes 1048592 | tf_op jit(solution)/shard_map/all_gather | solution.py:272
  58.0 0.0 copy-done.1
  58.0 0.0 copy-start
  58.0 1.2 copy-done
  59.2 3.8 %tile.1 = (f32[512,1024]{1,0:T(8,128)S(1)}, bf16[1024,512]{1,0:T(8,128)(2,1)S(1)}, f32[32,1,1024]{2,1,0:T(1,128)S(1)}, f32[1,1024]{1,0:T(1,128)S(1)}, f32[1,1024...) custom-call(f32[1]{0:T(128)S(6)} %exp.3.refs_0_, s32[1]{0:T(128)} %bitcast.refs_1_, ...), custom_call_target="tpu_custom_call" | custom-call | flops 1073741824 | bytes 6291456 | tf_op jit(solution)/shard_map/tile/pallas_call | solution.py:62
  63.1 18.3 %all_to_all.30.refs_0_ = f32[32,1,1024]{2,1,0:T(1,128)S(1)} all-to-all(f32[32,1,1024]{2,1,0:T(1,128)S(1)} %get-tuple-element.25), channel_id=1, replica_groups=mesh['img'=16,'txt'=32] {'txt'}, dimensions={0} | all-to-all | bytes 262144 | tf_op jit(solution)/shard_map/all_to_all | solution.py:31
  81.4 0.2 rows.1
  81.6 16.1 %all_to_all.31.refs_3_ = f32[16,1,1152]{2,1,0:T(1,128)S(1)} all-to-all(f32[16,1,1152]{2,1,0:T(1,128)S(1)} %get-tuple-element.31), channel_id=1, replica_groups=mesh['img'=16,'txt'=32] {'img'}, dimensions={0} | all-to-all | bytes 147456 | tf_op jit(solution)/shard_map/all_to_all | solution.py:31
  97.7 3.1 %weights.1 = (bf16[512,1024]{1,0:T(8,128)(2,1)S(1)}, bf16[8,136,1024]{2,1,0:T(8,128)(2,1)}) custom-call(f32[1]{0:T(128)S(6)} %exp.3.refs_0_, s32[1]{0:T(128)} %bitcast.refs_1_, s32[1,1024]{1,0:T(1,128)S(1)} %bitcast.10, f32[16,1,1152]{2,1,0:T(1,128)S(1)} %all_to_all.31.refs_3_, f32[1,1024]{1,0:T(1,128)S(1)} %get-tuple-element.32.refs_4_, ...), custom_call_target="tpu_custom_call" | custom-call | flops 1073741824 | bytes 6291456 | tf_op jit(solution)/shard_map/weights/pallas_call | solution.py:62
  100.8 3.6 %all-to-all-start.4 = ((bf16[8,136,1024]{2,1,0:T(8,128)(2,1)}), bf16[8,136,1024]{2,1,0:T(8,128)(2,1)S(1)}, u32[]{:S(2)}, u32[]{:S(2)}) async-start(bf16[8,136,1024]{2,1,0:T(8,128)(2,1)} %get-tuple-element.35), calls=%async_computation.4 | async-start | bytes 4456448 | tf_op jit(solution)/shard_map/all_to_all | solution.py:31
  104.4 0.0 reduce-scatter.2.cloned.1.call-start
  104.5 2.9 %texts.1 = (bf16[8,64,512]{2,1,0:T(8,128)(2,1)S(1)}, bf16[8,64,512]{2,1,0:T(8,128)(2,1)S(1)}) custom-call(f32[1]{0:T(128)S(6)} %exp.3.refs_0_, s32[1]{0:T(128)} %bitcast.6.refs_1_, bf16[512,1024]{1,0:T(8,128)(2,1)S(1)} %get-tuple-element.38.refs_2_, bf16[8,4,32,1024]{3,2,1,0:T(8,128)(2,1)} %get-tuple-element.42.refs_3_), custom_call_target="tpu_custom_call" | custom-call | flops 1073741824 | bytes 4194304 | tf_op jit(solution)/shard_map/texts/pallas_call | solution.py:62
  107.4 2.0 %collective-permute-start = (bf16[8,64,512]{2,1,0:T(8,128)(2,1)S(1)}, bf16[8,64,512]{2,1,0:T(8,128)(2,1)S(1)}, u32[]{:S(2)}, u32[]{:S(2)}) collective-permute-start(bf16[8,64,512]{2,1,0:T(8,128)(2,1)S(1)} %get-tuple-element.40), channel_id=1, source_target_pairs={{0,32},{32,0},{64,96},{96,64},{128,160},{160,128},{192,224},{224,1... | collective-permute-start | bytes 1572872 | tf_op jit(solution)/shard_map/ppermute | solution.py:334
  109.4 1.8 %collective-permute-done = bf16[8,64,512]{2,1,0:T(8,128)(2,1)S(1)} collective-permute-done((bf16[8,64,512]{2,1,0:T(8,128)(2,1)S(1)}, bf16[8,64,512]{2,1,0:T(8,128)(2,1)S(1)}, u32[]{:S(2)}, u32[]{:S(2)}) %collective-permute-start) | collective-permute-done | bytes 524320 | tf_op jit(solution)/shard_map/ppermute | solution.py:334
  111.2 0.9 add_convert_fusion
  112.1 0.0 reduce-scatter.2.cloned.1.call-update
  112.1 20.7 %all-to-all-done.4.refs_0_ = bf16[8,136,1024]{2,1,0:T(8,128)(2,1)S(1)} async-done(((bf16[8,136,1024]{2,1,0:T(8,128)(2,1)}), bf16[8,136,1024]{2,1,0:T(8,128)(2,1)S(1)}, u32[]{:S(2)}, u32[]{:S(2)}) %all-to-all-start.4) | async-done | bytes 2228256 | tf_op jit(solution)/shard_map/all_to_all | solution.py:31
  132.8 0.4 square.1
  133.2 12.6 %all_to_all.32.refs_0_ = bf16[4,32,1152]{2,1,0:T(8,128)(2,1)S(1)} all-to-all(bf16[4,32,1152]{2,1,0:T(8,128)(2,1)S(1)} %square.1), channel_id=1, replica_groups={{0,2,4,6},{1,3,5,7},{8,10,12,14},{9,11,13,15},{16,18,20,22},{17,19,21,2..., dimensions={0} | all-to-all | bytes 589824 | tf_op jit(solution)/shard_map/all_to_all | solution.py:31
  145.8 0.7 pair.1
  146.5 0.0 reduce-scatter.2.cloned.1.call-done
  (1 shorter events, 0.0 us)
Async XLA Ops:
  7.2 50.8 %all-gather.2.cloned.1.call-start = ((), (), s32[]{:S(2)}) async-start(), calls=%async_computation.7 | async-start | bytes 1114112 | tf_op jit(solution)/shard_map/all_gather | solution.py:272
  8.6 49.4 %copy-start.1 = (s32[1024]{0:T(1024)S(1)}, s32[1024]{0:T(1024)}, u32[]{:S(2)}) copy-start(s32[1024]{0:T(1024)} %param.8) | copy-start | bytes 12292
  58.0 1.2 copy-start
  100.8 32.1 %all-to-all-start.4 = ((bf16[8,136,1024]{2,1,0:T(8,128)(2,1)}), bf16[8,136,1024]{2,1,0:T(8,128)(2,1)S(1)}, u32[]{:S(2)}, u32[]{:S(2)}) async-start(bf16[8,136,1024]{2,1,0:T(8,128)(2,1)} %get-tuple-element.35), calls=%async_computation.4 | async-start | bytes 4456448 | tf_op jit(solution)/shard_map/all_to_all | solution.py:31
  104.4 42.1 %reduce-scatter.2.cloned.1.call-start = ((), (), s32[]{:S(2)}) async-start(), calls=%async_computation.8 | async-start | bytes 589824 | tf_op jit(solution)/shard_map/reduce_scatter | solution.py:335
  107.4 3.8 %collective-permute-start = (bf16[8,64,512]{2,1,0:T(8,128)(2,1)S(1)}, bf16[8,64,512]{2,1,0:T(8,128)(2,1)S(1)}, u32[]{:S(2)}, u32[]{:S(2)}) collective-permute-start(bf16[8,64,512]{2,1,0:T(8,128)(2,1)S(1)} %get-tuple-element.40), channel_id=1, source_target_pairs={{0,32},{32,0},{64,96},{96,64},{128,160},{160,128},{192,224},{224,1... | collective-permute-start | bytes 1572872 | tf_op jit(solution)/shard_map/ppermute | solution.py:334
Sparse Core Ops, SparseCore 0:
  10.1 47.8 all-gather.1
  112.2 29.4 reduce-scatter.1

commit v9 on v8

--- a/solution.py
+++ b/solution.py
@@ -103,11 +103,20 @@
 
 
 def tile_kernel(
-    scale_ref, base_ref, pos_ref, image_ref, text_ref,
+    scale_ref, base_ref, pos_ref, image_in, text_ref,
     logit_ref, text_out, row_out, row_norm, row_mean, col_norm, col_mean, matched_out,
+    image_ref, image_sems,
 ):
     depth, cols = text_ref.shape
     rows = pos_ref.shape[1]
+    half = SQUARE // 2
+    reads = []
+    for k in range(2):
+        span = pl.ds(k * half, half)
+        reads.append(
+            pltpu.make_async_copy(image_in.at[span], image_ref.at[span], image_sems.at[k])
+        )
+        reads[-1].start()
     part = depth // (SQUARE * Y_PAIRS)
     for x in range(X_CHIPS):
         for side in range(2):
@@ -115,14 +124,25 @@
                 source = ((x * Y_PAIRS + pair) * 2 + side) * part
                 target = ((x * 2 + side) * Y_PAIRS + pair) * part
                 text_out[target : target + part, :] = text_ref[source : source + part, :]
-    image_t = image_ref[...].reshape(depth, rows)
+    reads[0].wait()
+    image_t = image_ref[:half].reshape(depth // 2, rows)
+    for start in range(0, cols, LANES):
+        span = slice(start, start + LANES)
+        logit_ref[span, :] = lax.dot_general(
+            text_out[: depth // 2, span], image_t, (((0,), (0,)), ((), ())),
+            preferred_element_type=F32,
+        )
+    reads[1].wait()
+    image_t = image_ref[half:].reshape(depth // 2, rows)
     row_high = jnp.full((1, rows), -jnp.inf, F32)
     matched = jnp.zeros((1, rows), F32)
     for start in range(0, cols, LANES):
         span = slice(start, start + LANES)
-        logits = scale_ref[0] * lax.dot_general(
-            text_out[:, span], image_t, (((0,), (0,)), ((), ())), preferred_element_type=F32
-        )
+        logits = lax.dot_general(
+            text_out[depth // 2 :, span], image_t, (((0,), (0,)), ((), ())),
+            preferred_element_type=F32,
+        )
+        logits = scale_ref[0] * (logit_ref[span, :] + logits)
         logit_ref[span, :] = logits
         high = jnp.max(logits, axis=1, keepdims=True)
         powers = jnp.exp(logits - high)
@@ -285,7 +305,7 @@
     logits, text_t, row_out, row_norm, row_mean, col_norm, col_mean, matched = call(
         lambda *refs: tile_kernel(*refs),
         "tile",
-        [smem(), smem(), vmem(), vmem(), vmem()],
+        [smem(), smem(), vmem(), hbm(), vmem()],
         [
             ((cols, rows), F32, vmem()),
             ((depth, cols), BF16, vmem()),
@@ -297,6 +317,7 @@
             ((1, LANES), F32, vmem()),
         ],
         2 * macs, 6 << 20, 2 * rows * cols,
+        [pltpu.VMEM(image_full.shape, BF16), pltpu.SemaphoreType.DMA((2,))],
     )(scale, base, places, image_full, text_full)
 
     seen = exchange(row_out, "txt")

time: 155 us -> 154 us (level)
  no operation moved by 1% of the time
where the time goes in v9:
time: 154 us; the launch traced here: 152 us
  blocking collectives  90.9 us (59%)
  waiting for transfers between devices  26.7 us (17%)
  between operations  14.8 us (10%)
  Pallas kernels  11 us (7%)
  starting transfers between devices  5.73 us (4%)
  local copies, waits for them, and re-layouts  2.34 us (2%)
    all_to_all x5, blocking collectives, exchange(): return lax.all_to_all(blocks, axis, 0, 0, axis_index_groups=groups)  90.9 us
    all_to_all x1, waiting for transfers between devices, exchange(): return lax.all_to_all(blocks, axis, 0, 0, axis_index_groups=groups)  20.6 us
    pallas_call x6, Pallas kernels, call(): return lambda *operands: tuple(run(*operands))  11 us
    all_to_all x1, starting transfers between devices, exchange(): return lax.all_to_all(blocks, axis, 0, 0, axis_index_groups=groups)  3.62 us
    all_gather x1, waiting for transfers between devices, per_device(): text_full = lax.all_gather(texts.T, 'img', axis=0, tiled=True)  3.57 us
  transfers between devices with their start and end apart: 4, of which 3 were waited for; matrix products, arithmetic and copies ran while one was open for 1% of the time, Pallas kernels for 3%

profile of v9, /device:TPU:1, one launch (start us, length us, event | category | flops | bytes accessed | tf_op | source)
XLA Modules:
  0.0 152.4 jit_solution(6017854678439391641)
XLA Ops:
  7.2 0.0 all-gather.2.cloned.1.call-start
  7.2 0.7 all-gather.2.cloned.1.call-update
  8.6 0.0 copy-start.1
  8.6 45.8 %conditional.1 = (bf16[8,4,32,1024]{3,2,1,0:T(8,128)(2,1)}) conditional(s32[]{:T(128)} %bitcast.2, () %tuple.14, bf16[32,1024]{1,0:T(8,128)(2,1)} %bitcast.12), branch_computations={%region_0.1_spmd, %region_1.2_spmd} | conditional | bytes 7405576 | solution.py:302
  8.6 0.9 broadcast_in_dim.0
  9.5 16.5 %all_to_all.28 = bf16[4,32,1024]{2,1,0:T(8,128)(2,1)S(1)} all-to-all(bf16[4,32,1024]{2,1,0:T(8,128)(2,1)S(1)} %broadcast_in_dim.0), channel_id=1, replica_groups={{0,2,4,6},{1,3,5,7},{8,10,12,14},{9,11,13,15},{16,18,20,22},{17,19,21,2..., dimensions={0} | all-to-all | bytes 524288 | tf_op jit(solution)/shard_map/cond/branch_1_fun/all_to_all | solution.py:31
  25.9 0.3 broadcast_in_dim.1
  26.2 28.2 %all_to_all.29.block_ref = bf16[8,4,32,1024]{3,2,1,0:T(8,128)(2,1)} all-to-all(bf16[8,4,32,1024]{3,2,1,0:T(8,128)(2,1)S(1)} %broadcast_in_dim.1), channel_id=1, replica_groups={{0,1,8,9,16,17,24,25},{2,3,10,11,18,19,26,27},{4,5,12,13,20,21,28,29},{..., dimensions={0} | all-to-all | bytes 4194304 | tf_op jit(solution)/shard_map/cond/branch_1_fun/all_to_all | solution.py:31
  54.4 3.6 %all-gather.2.cloned.1.call-done.refs_4_ = bf16[1024,512]{1,0:T(8,128)(2,1)} async-done(((bf16[64,512]{1,0:T(8,128)(2,1)}), bf16[1024,512]{1,0:T(8,128)(2,1)}) %all-gather.2.cloned.1.call-update) | async-done | bytes 1048592 | tf_op jit(solution)/shard_map/all_gather | solution.py:292
  58.0 0.0 copy-done.1
  58.0 0.0 copy-start
  58.0 1.2 copy-done
  59.2 3.8 %tile.1 = (f32[512,1024]{1,0:T(8,128)S(1)}, bf16[1024,512]{1,0:T(8,128)(2,1)S(1)}, f32[32,1,1024]{2,1,0:T(1,128)S(1)}, f32[1,1024]{1,0:T(1,128)S(1)}, f32[1,1024...) custom-call(f32[1]{0:T(128)S(6)} %exp.3.refs_0_, s32[1]{0:T(128)} %bitcast.refs_1_, ...), custom_call_target="tpu_custom_call" | custom-call | flops 1073741824 | bytes 6291456 | tf_op jit(solution)/shard_map/tile/pallas_call | solution.py:62
  63.0 18.3 %all_to_all.30.refs_0_ = f32[32,1,1024]{2,1,0:T(1,128)S(1)} all-to-all(f32[32,1,1024]{2,1,0:T(1,128)S(1)} %get-tuple-element.25), channel_id=1, replica_groups=mesh['img'=16,'txt'=32] {'txt'}, dimensions={0} | all-to-all | bytes 262144 | tf_op jit(solution)/shard_map/all_to_all | solution.py:31
  81.3 0.2 rows.1
  81.5 16.1 %all_to_all.31.refs_3_ = f32[16,1,1152]{2,1,0:T(1,128)S(1)} all-to-all(f32[16,1,1152]{2,1,0:T(1,128)S(1)} %get-tuple-element.31), channel_id=1, replica_groups=mesh['img'=16,'txt'=32] {'img'}, dimensions={0} | all-to-all | bytes 147456 | tf_op jit(solution)/shard_map/all_to_all | solution.py:31
  97.6 3.0 %weights.1 = (bf16[512,1024]{1,0:T(8,128)(2,1)S(1)}, bf16[8,136,1024]{2,1,0:T(8,128)(2,1)}) custom-call(f32[1]{0:T(128)S(6)} %exp.3.refs_0_, s32[1]{0:T(128)} %bitcast.refs_1_, s32[1,1024]{1,0:T(1,128)S(1)} %bitcast.10, f32[16,1,1152]{2,1,0:T(1,128)S(1)} %all_to_all.31.refs_3_, f32[1,1024]{1,0:T(1,128)S(1)} %get-tuple-element.32.refs_4_, ...), custom_call_target="tpu_custom_call" | custom-call | flops 1073741824 | bytes 6291456 | tf_op jit(solution)/shard_map/weights/pallas_call | solution.py:62
  100.7 3.6 %all-to-all-start.4 = ((bf16[8,136,1024]{2,1,0:T(8,128)(2,1)}), bf16[8,136,1024]{2,1,0:T(8,128)(2,1)S(1)}, u32[]{:S(2)}, u32[]{:S(2)}) async-start(bf16[8,136,1024]{2,1,0:T(8,128)(2,1)} %get-tuple-element.35), calls=%async_computation.4 | async-start | bytes 4456448 | tf_op jit(solution)/shard_map/all_to_all | solution.py:31
  104.3 0.0 reduce-scatter.2.cloned.1.call-start
  104.4 2.9 %texts.1 = (bf16[8,64,512]{2,1,0:T(8,128)(2,1)S(1)}, bf16[8,64,512]{2,1,0:T(8,128)(2,1)S(1)}) custom-call(f32[1]{0:T(128)S(6)} %exp.3.refs_0_, s32[1]{0:T(128)} %bitcast.6.refs_1_, bf16[512,1024]{1,0:T(8,128)(2,1)S(1)} %get-tuple-element.38.refs_2_, bf16[8,4,32,1024]{3,2,1,0:T(8,128)(2,1)} %get-tuple-element.42.refs_3_), custom_call_target="tpu_custom_call" | custom-call | flops 1073741824 | bytes 4194304 | tf_op jit(solution)/shard_map/texts/pallas_call | solution.py:62
  107.3 2.0 %collective-permute-start = (bf16[8,64,512]{2,1,0:T(8,128)(2,1)S(1)}, bf16[8,64,512]{2,1,0:T(8,128)(2,1)S(1)}, u32[]{:S(2)}, u32[]{:S(2)}) collective-permute-start(bf16[8,64,512]{2,1,0:T(8,128)(2,1)S(1)} %get-tuple-element.40), channel_id=1, source_target_pairs={{0,32},{32,0},{64,96},{96,64},{128,160},{160,128},{192,224},{224,1... | collective-permute-start | bytes 1572872 | tf_op jit(solution)/shard_map/ppermute | solution.py:355
  109.3 1.8 %collective-permute-done = bf16[8,64,512]{2,1,0:T(8,128)(2,1)S(1)} collective-permute-done((bf16[8,64,512]{2,1,0:T(8,128)(2,1)S(1)}, bf16[8,64,512]{2,1,0:T(8,128)(2,1)S(1)}, u32[]{:S(2)}, u32[]{:S(2)}) %collective-permute-start) | collective-permute-done | bytes 524320 | tf_op jit(solution)/shard_map/ppermute | solution.py:355
  111.1 0.9 add_convert_fusion
  112.0 0.0 reduce-scatter.2.cloned.1.call-update
  112.0 20.6 %all-to-all-done.4.refs_0_ = bf16[8,136,1024]{2,1,0:T(8,128)(2,1)S(1)} async-done(((bf16[8,136,1024]{2,1,0:T(8,128)(2,1)}), bf16[8,136,1024]{2,1,0:T(8,128)(2,1)S(1)}, u32[]{:S(2)}, u32[]{:S(2)}) %all-to-all-start.4) | async-done | bytes 2228256 | tf_op jit(solution)/shard_map/all_to_all | solution.py:31
  132.6 0.4 square.1
  133.0 11.8 %all_to_all.32.refs_0_ = bf16[4,32,1152]{2,1,0:T(8,128)(2,1)S(1)} all-to-all(bf16[4,32,1152]{2,1,0:T(8,128)(2,1)S(1)} %square.1), channel_id=1, replica_groups={{0,2,4,6},{1,3,5,7},{8,10,12,14},{9,11,13,15},{16,18,20,22},{17,19,21,2..., dimensions={0} | all-to-all | bytes 589824 | tf_op jit(solution)/shard_map/all_to_all | solution.py:31
  144.8 0.7 pair.1
  145.5 0.0 reduce-scatter.2.cloned.1.call-done
  (1 shorter events, 0.0 us)
Async XLA Ops:
  7.2 50.8 %all-gather.2.cloned.1.call-start = ((), (), s32[]{:S(2)}) async-start(), calls=%async_computation.7 | async-start | bytes 1114112 | tf_op jit(solution)/shard_map/all_gather | solution.py:292
  8.6 49.4 %copy-start.1 = (s32[1024]{0:T(1024)S(1)}, s32[1024]{0:T(1024)}, u32[]{:S(2)}) copy-start(s32[1024]{0:T(1024)} %param.8) | copy-start | bytes 12292
  58.0 1.2 copy-start
  100.7 32.0 %all-to-all-start.4 = ((bf16[8,136,1024]{2,1,0:T(8,128)(2,1)}), bf16[8,136,1024]{2,1,0:T(8,128)(2,1)S(1)}, u32[]{:S(2)}, u32[]{:S(2)}) async-start(bf16[8,136,1024]{2,1,0:T(8,128)(2,1)} %get-tuple-element.35), calls=%async_computation.4 | async-start | bytes 4456448 | tf_op jit(solution)/shard_map/all_to_all | solution.py:31
  104.3 41.2 %reduce-scatter.2.cloned.1.call-start = ((), (), s32[]{:S(2)}) async-start(), calls=%async_computation.8 | async-start | bytes 589824 | tf_op jit(solution)/shard_map/reduce_scatter | solution.py:356
  107.3 3.8 %collective-permute-start = (bf16[8,64,512]{2,1,0:T(8,128)(2,1)S(1)}, bf16[8,64,512]{2,1,0:T(8,128)(2,1)S(1)}, u32[]{:S(2)}, u32[]{:S(2)}) collective-permute-start(bf16[8,64,512]{2,1,0:T(8,128)(2,1)S(1)} %get-tuple-element.40), channel_id=1, source_target_pairs={{0,32},{32,0},{64,96},{96,64},{128,160},{160,128},{192,224},{224,1... | collective-permute-start | bytes 1572872 | tf_op jit(solution)/shard_map/ppermute | solution.py:355
Sparse Core Ops, SparseCore 0:
  10.1 47.8 all-gather.1
  112.2 29.4 reduce-scatter.1
